TPU v7x, 32 devices: a whole 2x2x4 slice. The times are simulated.
32 devices in a mesh: site: 16 (over z, y, x), batch: 2 (over core).
Axes of the slice: x: 2, y: 2, z: 4, core: 2. Of those that a mesh axis runs over, the one named last changes fastest.
Arguments:
- site_tensors: bfloat16 [16, 2, 32, 128, 128], P('site')
- start_vector: float32 [16, 128], P('batch'), may hold values from -6 to 6
- start_label: int32 [16], P('batch'), may hold values from 0 to 31
- occupations: int32 [16, 16], P('site', 'batch'), may hold values from 0 to 1
Outputs:
- fill_prob: float32 [16, 16], P('site', 'batch')
- mean_logprob: float32 [16], P('batch')
- site_fill: float32 [16], P('site')
All inputs are finite; a program needn't handle non-finite values.
Results may differ from a plain program's by a relative error of at most 0.0003.
Values sent between devices are 32-bit elements; how exact they have to be, the bound alone decides.
No kernel may reach another device: no remote copies, remote signals or barrier semaphores. Data moves between devices by JAX's collectives and lax.ppermute only.
A program may use at most 128 MiB of HBM per device.

v0:
```python
import jax
import jax.numpy as jnp
from jax import lax
from jax.sharding import PartitionSpec as P

epsilon = 1e-06


def prefix_2(part, axis, combine, identity):
    place = lax.axis_index(axis)
    gathered = lax.all_gather(part, axis)
    state = jnp.zeros_like(part) + jnp.asarray(identity, part.dtype)

    def one(turn, state):
        return combine(state, lax.dynamic_index_in_dim(gathered, turn, 0, False))

    return lax.fori_loop(0, place, one, state)


def add_counts(earlier_part, later_part):
    return earlier_part + later_part


def compose(earlier_part, later_part):
    return lax.dot_general(
        earlier_part,
        later_part,
        (((2,), (1,)), ((0,), (0,))),
        precision=lax.Precision.HIGHEST,
        preferred_element_type=jnp.float32,
    )


def earlier_products(matrices):
    identity = jnp.broadcast_to(jnp.eye(matrices.shape[1], dtype=jnp.float32), matrices.shape)
    return prefix_2(matrices, "site", compose, identity)


def on_device(site_tensors, start_vector, start_label, occupations):
    sectors = site_tensors.shape[2]
    width = site_tensors.shape[3]
    block_table = site_tensors.reshape(2 * sectors, width, width)
    occupied = occupations[0]
    samples_here = occupied.shape[0]
    earlier = prefix_2(occupied, "site", add_counts, jnp.zeros_like(occupied))
    sector_label = ((start_label + earlier) % sectors).astype(jnp.int32)
    zero_blocks = jnp.take(block_table, sector_label, axis=0)
    one_blocks = jnp.take(block_table, sector_label + sectors, axis=0)
    chosen_blocks = jnp.where((occupied == 1)[:, None, None], one_blocks, zero_blocks).astype(
        jnp.float32
    )
    pieces = earlier_products(chosen_blocks)
    vector = jnp.einsum("sa,sab->sb", start_vector, pieces, precision=lax.Precision.HIGHEST)
    w_zero = jnp.einsum(
        "sa,sab->sb", vector, zero_blocks.astype(jnp.float32), precision=lax.Precision.HIGHEST
    )
    w_one = jnp.einsum(
        "sa,sab->sb", vector, one_blocks.astype(jnp.float32), precision=lax.Precision.HIGHEST
    )
    e_zero = jnp.sum(w_zero * w_zero, axis=1)
    e_one = jnp.sum(w_one * w_one, axis=1)
    total = e_zero + e_one + epsilon
    fill_probs = e_one / total
    chosen = jnp.where(occupied == 1, e_one, e_zero)
    log_term = jnp.log(chosen + epsilon) - jnp.log(total)
    site_count = lax.axis_size("site")
    batch_count = lax.axis_size("batch")
    loglik_total = lax.psum(log_term, "site")
    fill_total = lax.psum(jnp.sum(fill_probs)[None], "batch")
    mean_logprob = loglik_total / site_count
    site_fill = fill_total / (samples_here * batch_count)
    return (fill_probs[None, :], mean_logprob, site_fill)


def solution(mesh):
    placed = (P("site", None, None, None, None), P("batch", None), P("batch"), P("site", "batch"))
    return jax.shard_map(
        on_device,
        mesh=mesh,
        in_specs=placed,
        out_specs=(P("site", "batch"), P("batch"), P("site")),
        check_vma=False,
    )
```

profile of v0, /device:TPU:0, one launch (start us, length us, event | category | flops | bytes accessed | tf_op | source)
XLA Modules:
  0.0 248.8 jit_solution(4046141666863826744)
XLA Ops:
  7.2 0.0 copy-start
  7.2 0.0 all-gather.4.cloned.1.call-start
  7.2 0.8 compare_bitcast_fusion
  8.0 42.3 %all-gather.1 = s32[16,1,8]{2,1,0:T(1,128)S(1)} all-gather(s32[1,1,8]{2,1,0:T(1,128)} %bitcast.58), channel_id=1, replica_groups=mesh['site'=16,'batch'=2] {'site'}, dimensions={0}, use_global_device_ids=true | all-gather | bytes 544 | tf_op jit(solution)/shard_map/all_gather | solution.py:11
  50.4 0.0 copy-start.1
  50.4 0.7 compare_and_fusion
  51.1 0.0 copy-done
  51.1 0.6 gather_fusion.1
  51.7 0.6 gather_fusion
  52.3 0.0 copy-start.2
  52.3 1.0 select_convert_fusion
  53.3 0.0 all-gather.4.cloned.1.call-update
  53.4 109.1 %all-gather.4.cloned.1.call-done = f32[128,128,128]{2,1,0:T(8,128)} async-done(((f32[8,128,128]{2,1,0:T(8,128)}), f32[128,128,128]{2,1,0:T(8,128)}) %all-gather.4.cloned.1.call-update) | async-done | bytes 8388624 | tf_op jit(solution)/shard_map/all_gather | solution.py:11
  162.5 0.0 copy-done.1
  162.5 0.9 convolution_bitcast_fusion.1
  163.4 0.4 fusion.4
  163.8 0.4 fusion.3
  164.2 0.2 multiply_reduce_fusion
  164.4 0.5 fusion.8
  164.9 0.0 copy-done.2
  164.9 0.6 divide_reduce_fusion
  165.5 3.1 %psum.15 = f32[1]{0:T(128)} all-reduce(f32[1]{0:T(128)} %bitcast.21), channel_id=1, replica_groups=mesh['site'=16,'batch'=2] {'batch'}, use_global_device_ids=true, to_apply=%region_8.10 | all-reduce | flops 1 | bytes 8 | tf_op jit(solution)/shard_map/psum | solution.py:69
  168.6 71.1 %psum.14 = f32[8]{0:T(128)S(1)} all-reduce(f32[8]{0:T(128)S(1)} %get-tuple-element.101), channel_id=1, replica_groups=mesh['site'=16,'batch'=2] {'site'}, use_global_device_ids=true, to_apply=%region_6.8 | all-reduce | flops 8 | bytes 64 | tf_op jit(solution)/shard_map/psum | solution.py:68
  239.7 0.5 broadcast_multiply_fusion
  (9 shorter events, 0.1 us)
Async XLA Ops:
  7.2 43.9 %copy-start = (bf16[1,2,32,128,128]{4,3,2,1,0:T(8,128)(2,1)S(1)}, bf16[1,2,32,128,128]{4,3,2,1,0:T(8,128)(2,1)}, u32[]{:S(2)}) copy-start(bf16[1,2,32,128,128]{4,3,2,1,0:T(8,128)(2,1)} %param.10) | copy-start | bytes 6291460
  7.2 155.2 %all-gather.4.cloned.1.call-start = ((), (), s32[]{:S(2)}) async-start(), calls=%async_computation | async-start | bytes 8912896 | tf_op jit(solution)/shard_map/all_gather | solution.py:11
  50.4 112.1 %copy-start.1 = (f32[8,128]{1,0:T(8,128)S(1)}, f32[8,128]{1,0:T(8,128)}, u32[]{:S(2)}) copy-start(f32[8,128]{1,0:T(8,128)} %param.11) | copy-start | bytes 12292
  52.3 112.6 %copy-start.2 = (s32[1,8]{1,0:T(1,128)S(1)}, s32[1,8]{1,0:T(1,128)}, u32[]{:S(2)}) copy-start(s32[1,8]{1,0:T(1,128)} %param.13) | copy-start | bytes 100
Sparse Core Ops, SparseCore 0:
  53.5 108.9 all-gather.3
where the time goes:
time: 250 us; the launch traced here: 249 us
  blocking collectives  116 us (46%)
  waiting for transfers between devices  109 us (44%)
  between operations  15.9 us (6%)
  other arithmetic  4.32 us (2%)
    all_gather x1, waiting for transfers between devices, prefix_2(): gathered = lax.all_gather(part, axis)  109 us
    psum x1, blocking collectives, on_device(): loglik_total = lax.psum(log_term, 'site')  71.1 us
    all_gather x1, blocking collectives, prefix_2(): gathered = lax.all_gather(part, axis)  42.3 us
  transfers between devices with their start and end apart: 1, of which 1 were waited for; matrix products, arithmetic and copies ran while one was open for 0% of the time, Pallas kernels for 0%

commit v1 on v0

v1 whole, which is shorter than its diff:
```python
import functools

import jax
import jax.numpy as jnp
from jax import lax
from jax.experimental import pallas as pl
from jax.experimental.pallas import tpu as pltpu
from jax.sharding import PartitionSpec as P

epsilon = 1e-06
LANES = 128


def fetch_kernel(picks, table, out, held, sems):
    samples = out.shape[0]
    copies = [
        pltpu.make_async_copy(table.at[picks[n, s]], held.at[s, n], sems.at[s, n])
        for s in range(samples)
        for n in range(2)
    ]
    for copy in copies:
        copy.start()
    at = 0
    for s in range(samples):
        for n in range(2):
            copies[at].wait()
            at += 1
            out[s, n] = held[s, n].astype(jnp.float32)


def fetch_blocks(picks, table):
    samples = picks.shape[1]
    width = table.shape[-1]
    shape = (samples, 2, width, width)
    return pl.pallas_call(
        fetch_kernel,
        grid_spec=pltpu.PrefetchScalarGridSpec(
            num_scalar_prefetch=1,
            grid=(1,),
            in_specs=[pl.BlockSpec(memory_space=pl.ANY)],
            out_specs=pl.BlockSpec(shape, lambda i, picks: (0, 0, 0, 0)),
            scratch_shapes=[
                pltpu.VMEM(shape, table.dtype),
                pltpu.SemaphoreType.DMA((samples, 2)),
            ],
        ),
        out_shape=jax.ShapeDtypeStruct(shape, jnp.float32),
        compiler_params=pltpu.CompilerParams(vmem_limit_bytes=16 << 20),
        name="fetch_blocks",
    )(picks, table)


def halves(x):
    high = x.astype(jnp.bfloat16)
    low = (x - high.astype(jnp.float32)).astype(jnp.bfloat16)
    return high, low


def times_block(left, block):
    high, low = halves(left)
    rows = left.shape[0]
    both = jnp.dot(
        jnp.concatenate([high, low], axis=0), block, preferred_element_type=jnp.float32
    )
    return both[:rows] + both[rows:]


def as_column(row):
    width = row.shape[-1]
    return jnp.broadcast_to(row, (width, width)).T


def products_kernel(blocks, start, out, leaving):
    steps = blocks.shape[0]
    left = None
    for k in range(steps):
        chosen = blocks[k, 0]
        other = blocks[k, 1]
        if left is None:
            out[0, 1] = other
            left = chosen
        else:
            out[k, 1] = times_block(left, other.astype(jnp.bfloat16))
            left = times_block(left, chosen.astype(jnp.bfloat16))
        out[k, 0] = left
    leaving[...] = jnp.sum(as_column(start[0:1, :]) * left, axis=0, keepdims=True)


def group_products(blocks, start):
    whole = pl.BlockSpec(memory_space=pltpu.VMEM)
    return pl.pallas_call(
        products_kernel,
        in_specs=[whole, whole],
        out_specs=[whole, whole],
        out_shape=[
            jax.ShapeDtypeStruct(blocks.shape, jnp.float32),
            jax.ShapeDtypeStruct((1, blocks.shape[-1]), jnp.float32),
        ],
        compiler_params=pltpu.CompilerParams(vmem_limit_bytes=16 << 20),
        name="group_products",
    )(blocks, start)


def weights_kernel(products, vector, out):
    steps = products.shape[0]
    column = as_column(vector[...])
    for k in range(steps):
        for n in range(2):
            row = jnp.sum(column * products[k, n], axis=0, keepdims=True)
            total = jnp.sum(row * row, axis=1, keepdims=True)
            out[n, k : k + 1, :] = jnp.broadcast_to(total, (1, LANES))


def group_weights(products, vector):
    whole = pl.BlockSpec(memory_space=pltpu.VMEM)
    return pl.pallas_call(
        weights_kernel,
        in_specs=[whole, whole],
        out_specs=whole,
        out_shape=jax.ShapeDtypeStruct((2, products.shape[0], LANES), jnp.float32),
        compiler_params=pltpu.CompilerParams(vmem_limit_bytes=16 << 20),
        name="group_weights",
    )(products, vector)


def on_device(site_tensors, start_vector, start_label, occupations):
    sectors = site_tensors.shape[2]
    width = site_tensors.shape[3]
    sites = lax.axis_size("site")
    batches = lax.axis_size("batch")
    samples = occupations.shape[1]
    group = samples
    groups = sites // group
    everyone = sites * batches
    place = lax.axis_index("site")
    batch = lax.axis_index("batch")
    mine = place % group
    here = place // group

    table = site_tensors.reshape(2 * sectors, width, width)
    occupied = occupations[0]

    row = jnp.pad(occupied, (0, LANES - samples))[None, :]
    heard = lax.all_to_all(
        jnp.broadcast_to(row, (everyone, LANES)), ("site", "batch"), 0, 0, tiled=True
    )
    heard = heard.reshape(sites, batches, LANES)
    all_occupied = lax.dynamic_index_in_dim(heard, batch, 1, False)[:, :samples]
    before = (jnp.arange(sites) < place)[:, None]
    earlier = jnp.sum(jnp.where(before, all_occupied, 0), axis=0)
    label = (start_label + earlier) % sectors
    picks = jnp.stack([label + sectors * occupied, label + sectors * (1 - occupied)])

    blocks = fetch_blocks(picks, table)
    teams = [[g * group + k for k in range(group)] for g in range(groups)]
    blocks = lax.all_to_all(blocks, "site", 0, 0, tiled=True, axis_index_groups=teams)

    start = lax.dynamic_slice_in_dim(start_vector, mine, 1, 0)
    products, leaving = group_products(blocks, start)

    vector = start
    onward = [(i, (i + group) % sites) for i in range(sites)]
    for turn in range(1, groups):
        if turn > 1:
            leaving = jnp.einsum(
                "sa,ab->sb", vector, products[-1, 0], precision=lax.Precision.HIGHEST
            )
        arrived = lax.ppermute(leaving, "site", onward)
        vector = jnp.where(here == turn, arrived, vector)

    found = group_weights(products, vector)[:, :, 0]
    of_chosen, of_other = found[0], found[1]
    group_occupied = lax.dynamic_slice(all_occupied, (here * group, mine), (group, 1))[:, 0]
    e_one = jnp.where(group_occupied == 1, of_chosen, of_other)
    total = of_chosen + of_other + epsilon
    fill = e_one / total
    log_sum = jnp.sum(jnp.log(of_chosen + epsilon) - jnp.log(total))

    fill_of_site = jnp.zeros((groups, group), jnp.float32)
    fill_of_site = jnp.where((jnp.arange(groups) == here)[:, None], fill[None, :], 0.0)
    fill_of_site = jnp.repeat(fill_of_site.reshape(sites), batches)
    lane = jnp.arange(LANES)[None, :]
    message = jnp.where(
        lane == 0, fill_of_site[:, None], jnp.where(lane == 1, log_sum, 0.0)
    ).astype(jnp.float32)
    reply = lax.all_to_all(message, ("site", "batch"), 0, 0, tiled=True)
    reply = reply.reshape(groups, group, batches, LANES)
    own = lax.dynamic_index_in_dim(reply, batch, 2, False)
    fill_probs = jnp.sum(own[:, :, 0], axis=0)
    mean_logprob = jnp.sum(own[:, :, 1], axis=0) / sites
    site_fill = jnp.sum(reply[:, :, :, 0])[None] / (samples * batches)
    return (fill_probs[None, :], mean_logprob, site_fill)


def solution(mesh):
    placed = (P("site", None, None, None, None), P("batch", None), P("batch"), P("site", "batch"))
    return jax.shard_map(
        on_device,
        mesh=mesh,
        in_specs=placed,
        out_specs=(P("site", "batch"), P("batch"), P("site")),
        check_vma=False,
    )
```

time: 250 us -> 61.9 us (0.25)
  blocking collectives: 116 us -> 9.38 us
  waiting for transfers between devices: 109 us -> 25 us
  between operations: 15.9 us -> 2.52 us
  starting transfers between devices: 0.04 us -> 11.4 us
  Pallas kernels: 0 us -> 3.75 us
  local copies, waits for them, and re-layouts: 1.25 us -> 3.97 us
    all_gather x1 -> x0, waiting for transfers between devices: 109 us -> none  [prefix_2(): gathered = lax.all_gather(part, axis)]
    psum x2 -> x0, blocking collectives: 74.2 us -> none  [the longest x1 71.1 us: on_device(): loglik_total = lax.psum(log_term, 'site')]
    all_gather x1 -> x0, blocking collectives: 42.3 us -> none  [prefix_2(): gathered = lax.all_gather(part, axis)]
    all_to_all x0 -> x2, waiting for transfers between devices: none -> 21.2 us  [the longest x1 14.1 us: on_device(): lax.all_to_all(blocks, 'site', 0, 0, tiled=True, axis_index_groups=teams)]
    all_to_all x0 -> x2, starting transfers between devices: none -> 10.9 us  [the longest x1 7.3 us: on_device(): lax.all_to_all(jnp.broadcast_to(row, (everyone, LANES)), ('site', 'batch'...]
    all_to_all x0 -> x1, blocking collectives: none -> 9.38 us  [on_device(): reply = lax.all_to_all(message, ('site', 'batch'), 0, 0, tiled=True)]
    ppermute x0 -> x1, waiting for transfers between devices: none -> 3.77 us  [on_device(): arrived = lax.ppermute(leaving, 'site', onward)]
    pallas_call x0 -> x3, Pallas kernels: none -> 3.75 us  [the longest x1 2.47 us: fetch_blocks(): pl.pallas_call(fetch_kernel, grid_spec=pltpu.PrefetchScalarGridSpec(num_s...]
  transfers between devices with their start and end apart: 1 -> 3, of which waited for: 1 -> 3; matrix products, arithmetic and copies ran while one was open for 0% -> 1% of each run, Pallas kernels for 0% -> 0%
where the time goes in v1:
time: 61.9 us; the launch traced here: 61.5 us
  waiting for transfers between devices  25 us (40%)
  starting transfers between devices  11.4 us (18%)
  blocking collectives  9.38 us (15%)
  other arithmetic  5.54 us (9%)
  local copies, waits for them, and re-layouts  3.97 us (6%)
  Pallas kernels  3.75 us (6%)
  between operations  2.52 us (4%)
    all_to_all x1, waiting for transfers between devices, on_device(): lax.all_to_all(blocks, 'site', 0, 0, tiled=True, axis_index_groups=teams)  14.1 us
    all_to_all x1, blocking collectives, on_device(): reply = lax.all_to_all(message, ('site', 'batch'), 0, 0, tiled=True)  9.38 us
    all_to_all x1, starting transfers between devices, on_device(): lax.all_to_all(jnp.broadcast_to(row, (everyone, LANES)), ('site', 'batch'...  7.3 us
    all_to_all x1, waiting for transfers between devices, on_device(): lax.all_to_all(jnp.broadcast_to(row, (everyone, LANES)), ('site', 'batch'...  7.13 us
    ppermute x1, waiting for transfers between devices, on_device(): arrived = lax.ppermute(leaving, 'site', onward)  3.77 us
    all_to_all x1, starting transfers between devices, on_device(): lax.all_to_all(blocks, 'site', 0, 0, tiled=True, axis_index_groups=teams)  3.57 us
    pallas_call x1, Pallas kernels, fetch_blocks(): pl.pallas_call(fetch_kernel, grid_spec=pltpu.PrefetchScalarGridSpec(num_s...  2.47 us
    unnamed x2, local copies, waits for them, and re-layouts  1.58 us
  transfers between devices with their start and end apart: 3, of which 3 were waited for; matrix products, arithmetic and copies ran while one was open for 1% of the time, Pallas kernels for 0%

profile of v1, /device:TPU:0, one launch (start us, length us, event | category | flops | bytes accessed | tf_op | source)
XLA Modules:
  0.0 61.5 jit_solution(13478709235840130360)
XLA Ops:
  0.6 0.7 %pad.4 = s32[128]{0:T(128)S(1)} pad(s32[8]{0:T(128)} %bitcast.20, s32[]{:T(128)} %constant.60.clone.1), padding=0_120 | pad | bytes 548 | tf_op jit(solution)/shard_map/jit(_pad)/pad | solution.py:143
  1.3 0.6 broadcast_in_dim.85
  1.9 7.3 %all-to-all-start = ((s32[32,1,128]{2,1,0:T(1,128)}), s32[32,1,128]{2,1,0:T(1,128)S(1)}, u32[]{:S(2)}, u32[]{:S(2)}) async-start(s32[32,1,128]{2,1,0:T(1,128)} %broadcast_in_dim.85), calls=%async_computation | async-start | bytes 32768 | tf_op jit(solution)/shard_map/all_to_all | solution.py:144
  9.2 7.1 %all-to-all-done = s32[32,1,128]{2,1,0:T(1,128)S(1)} async-done(((s32[32,1,128]{2,1,0:T(1,128)}), s32[32,1,128]{2,1,0:T(1,128)S(1)}, u32[]{:S(2)}, u32[]{:S(2)}) %all-to-all-start) | async-done | bytes 16416 | tf_op jit(solution)/shard_map/all_to_all | solution.py:144
  16.4 0.1 fusion.2
  16.5 0.7 %add_bitcast_fusion.1 = (s32[1,8]{1,0:T(1,128)S(1)}, s32[8]{0:T(128)S(1)}) fusion(s32[1,8]{1,0:T(1,128)} %param.7, s32[8]{0:T(128)} %param.6, s32[8]{0:T(128)S(1)} %get-tuple-element.14), kind=kLoop, calls=%fused_computation.24 | loop fusion | flops 112 | bytes 160 | tf_op jit(solution)/shard_map/stack | solution.py:152
  17.1 0.7 %add_bitcast_fusion = s32[1,8]{1,0:T(1,128)S(1)} fusion(s32[8]{0:T(128)S(1)} %get-tuple-element.12, s32[1,8]{1,0:T(1,128)} %param.7), kind=kLoop, calls=%fused_computation.23 | loop fusion | flops 24 | bytes 96 | tf_op jit(solution)/shard_map/stack | solution.py:152
  17.8 0.0 copy-start
  17.8 1.6 %copy-done = bf16[1,2,32,128,128]{4,3,2,1,0:T(8,128)(2,1)S(1)} copy-done((bf16[1,2,32,128,128]{4,3,2,1,0:T(8,128)(2,1)S(1)}, bf16[1,2,32,128,128]{4,3,2,1,0:T(8,128)(2,1)}, u32[]{:S(2)}) %copy-start) | copy-done | bytes 2097176
  19.4 2.5 %fetch_blocks.1 = f32[8,2,128,128]{3,2,1,0:T(8,128)} custom-call(s32[2,8]{1,0:T(2,128)S(1)} %pad_add_fusion.picks, bf16[64,128,128]{2,1,0:T(8,128)(2,1)S(1)} %bitcast.14), custom_call_target="tpu_custom_call" | custom-call | tf_op jit(solution)/shard_map/fetch_blocks/pallas_call | solution.py:35
  21.9 3.6 %all-to-all-start.1 = ((f32[8,2,128,128]{3,2,1,0:T(8,128)}), f32[8,2,128,128]{3,2,1,0:T(8,128)S(1)}, u32[]{:S(2)}, u32[]{:S(2)}) async-start(f32[8,2,128,128]{3,2,1,0:T(8,128)} %fetch_blocks.1), calls=%async_computation.1 | async-start | bytes 2097152 | tf_op jit(solution)/shard_map/all_to_all | solution.py:156
  25.5 0.7 %constant_dynamic-slice_fusion.1.start = f32[1,128]{1,0:T(1,128)S(1)} fusion(f32[8,128]{1,0:T(8,128)} %param.5, s32[]{:T(128)S(6)} %select_n.82), kind=kLoop, calls=%fused_computation.17 | loop fusion | bytes 1028 | tf_op jit(solution)/shard_map/dynamic_slice | solution.py:158
  26.2 14.1 %all-to-all-done.1.blocks = f32[8,2,128,128]{3,2,1,0:T(8,128)S(1)} async-done(((f32[8,2,128,128]{3,2,1,0:T(8,128)}), f32[8,2,128,128]{3,2,1,0:T(8,128)S(1)}, u32[]{:S(2)}, u32[]{:S(2)}) %all-to-all-start.1) | async-done | bytes 1048608 | tf_op jit(solution)/shard_map/all_to_all | solution.py:156
  40.3 1.0 %group_products.1 = (f32[8,2,128,128]{3,2,1,0:T(8,128)S(1)}, f32[1,128]{1,0:T(1,128)S(1)}) custom-call(f32[8,2,128,128]{3,2,1,0:T(8,128)S(1)} %all-to-all-done.1.blocks, f32[1,128]{1,0:T(1,128)S(1)} %constant_dynamic-slice_fusion.1.start), custom_call_target="tpu_custom_call" | custom-call | tf_op jit(solution)/shard_map/group_products/pallas_call | solution.py:91
  41.3 0.5 collective-permute-start
  41.9 0.2 fusion
  42.1 3.8 %collective-permute-done = f32[1,128]{1,0:T(1,128)S(1)} collective-permute-done((f32[1,128]{1,0:T(1,128)S(1)}, f32[1,128]{1,0:T(1,128)S(1)}, u32[]{:S(2)}, u32[]{:S(2)}) %collective-permute-start) | collective-permute-done | bytes 544 | tf_op jit(solution)/shard_map/ppermute | solution.py:168
  45.8 0.7 %broadcast_select_fusion.1.vector = f32[1,128]{1,0:T(1,128)S(1)} fusion(f32[1,128]{1,0:T(1,128)S(1)} %collective-permute-done, pred[]{:T(512)S(6)} %eq.55, f32[8,128]{1,0:T(8,128)} %param.5, s32[]{:T(128)S(6)} %select_n.82), kind=kLoop, calls=%fused_computation.14 | loop fusion | flops 128 | bytes 1541 | tf_op jit(solution)/shard_map/jit(_where)/select_n | solution.py:169
  46.5 0.2 group_weights.1
  46.8 0.1 slice_reduce_fusion.3
  46.9 0.6 %select_divide_fusion = (f32[8]{0:T(128)S(1)}, f32[]{:T(128)}) fusion(pred[8]{0:T(512)(128)(4,1)S(1)} %fusion, f32[8]{0:T(128)S(1)} %get-tuple-element.10, f32[8]{0:T(128)S(1)} %get-tuple-element.9), kind=kLoop, calls=%fused_computation.22 | loop fusion | flops 55 | bytes 108 | tf_op jit(solution)/shard_map/div | solution.py:176
  47.5 0.6 %compare_select_fusion.2 = f32[128]{0:T(128)S(1)} fusion(f32[]{:T(128)} %get-tuple-element.16), kind=kLoop, calls=%fused_computation.11 | loop fusion | flops 256 | bytes 516 | tf_op jit(solution)/shard_map/jit(_where)/select_n | solution.py:184
  48.2 0.1 broadcast_select_fusion.2
  48.3 0.1 select_n.89
  48.3 0.1 broadcast_in_dim.90
  48.4 0.1 broadcast_in_dim.91
  48.5 0.1 broadcast_select_fusion
  48.6 9.4 %all_to_all.17 = f32[32,1,128]{2,1,0:T(1,128)S(1)} all-to-all(f32[32,1,128]{2,1,0:T(1,128)S(1)} %broadcast_select_fusion), channel_id=1, replica_groups=mesh['site'=16,'batch'=2] {'site','batch'}, dimensions={0} | all-to-all | bytes 32768 | tf_op jit(solution)/shard_map/all_to_all | solution.py:186
  58.0 0.6 %slice_reduce_fusion = f32[]{:T(128)} fusion(f32[2,8,2,128]{3,2,1,0:T(2,128)S(1)} %bitcast.16), kind=kLoop, calls=%fused_computation.1 | loop fusion | flops 31 | bytes 132 | tf_op jit(solution)/shard_map/reduce_sum | solution.py:191
  58.6 0.6 %slice_reduce_fusion.1 = (f32[8]{0:T(128)S(1)}, f32[8]{0:T(128)}) fusion(f32[2,8,128]{2,1,0:T(8,128)S(1)} %bitcast.17), kind=kLoop, calls=%fused_computation.2 | loop fusion | flops 16 | bytes 192 | tf_op jit(solution)/shard_map/reduce_sum | solution.py:190
  59.3 0.5 broadcast_multiply_fusion
  (6 shorter events, 0.0 us)
Async XLA Ops:
  1.9 14.4 %all-to-all-start = ((s32[32,1,128]{2,1,0:T(1,128)}), s32[32,1,128]{2,1,0:T(1,128)S(1)}, u32[]{:S(2)}, u32[]{:S(2)}) async-start(s32[32,1,128]{2,1,0:T(1,128)} %broadcast_in_dim.85), calls=%async_computation | async-start | bytes 32768 | tf_op jit(solution)/shard_map/all_to_all | solution.py:144
  17.8 1.6 %copy-start = (bf16[1,2,32,128,128]{4,3,2,1,0:T(8,128)(2,1)S(1)}, bf16[1,2,32,128,128]{4,3,2,1,0:T(8,128)(2,1)}, u32[]{:S(2)}) copy-start(bf16[1,2,32,128,128]{4,3,2,1,0:T(8,128)(2,1)} %param.4) | copy-start | bytes 6291460
  21.9 18.4 %all-to-all-start.1 = ((f32[8,2,128,128]{3,2,1,0:T(8,128)}), f32[8,2,128,128]{3,2,1,0:T(8,128)S(1)}, u32[]{:S(2)}, u32[]{:S(2)}) async-start(f32[8,2,128,128]{3,2,1,0:T(8,128)} %fetch_blocks.1), calls=%async_computation.1 | async-start | bytes 2097152 | tf_op jit(solution)/shard_map/all_to_all | solution.py:156
  41.3 4.5 %collective-permute-start = (f32[1,128]{1,0:T(1,128)S(1)}, f32[1,128]{1,0:T(1,128)S(1)}, u32[]{:S(2)}, u32[]{:S(2)}) collective-permute-start(f32[1,128]{1,0:T(1,128)S(1)} %get-tuple-element.6), channel_id=1, source_target_pairs={{0,16},{2,18},{4,20},{6,22},{8,24},{10,26},{12,28},{14,30},{16,0},... | collective-permute-start | bytes 1544 | tf_op jit(solution)/shard_map/ppermute | solution.py:168

commit v2 on v0

v2 whole, which is shorter than its diff:
```python
import jax
import jax.numpy as jnp
from jax import lax
from jax.experimental import pallas as pl
from jax.experimental.pallas import tpu as pltpu
from jax.sharding import PartitionSpec as P

epsilon = 1e-06
LANES = 128
VMEM_BYTES = 24 << 20


def whole():
    return pl.BlockSpec(memory_space=pltpu.VMEM)


def lanes_of(shape):
    return lax.broadcasted_iota(jnp.int32, shape, 1)


def rows_of(shape):
    return lax.broadcasted_iota(jnp.int32, shape, 0)


def tell_kernel(sites, group, occupied, out, row):
    place, batch = lax.axis_index("site"), lax.axis_index("batch")
    samples = occupied.shape[1]
    row[...] = jnp.zeros_like(row)
    row[0:1, 0:samples] = occupied[...]
    shape = out.shape
    occ = row[0:1, :]
    lane = lanes_of(shape)
    to = rows_of(shape)
    to_batch, to_site = to // sites, to % sites
    later = jnp.where(to_site > place, occ, 0)
    owned = jnp.sum(jnp.where(lane == to_site % group, occ, 0), axis=1, keepdims=True)
    message = jnp.where(lane < samples, later, jnp.where(lane == samples, owned, 0))
    out[...] = jnp.where(to_batch == batch, message, 0)


def keep_kernel(table, out, sem):
    copy = pltpu.make_async_copy(table, out, sem)
    copy.start()
    copy.wait()


def keep(table):
    return pl.pallas_call(
        keep_kernel,
        in_specs=[pl.BlockSpec(memory_space=pltpu.HBM)],
        out_specs=whole(),
        scratch_shapes=[pltpu.SemaphoreType.DMA],
        out_shape=jax.ShapeDtypeStruct(table.shape, table.dtype),
        compiler_params=pltpu.CompilerParams(vmem_limit_bytes=VMEM_BYTES),
        cost_estimate=pl.CostEstimate(flops=0, bytes_accessed=4 * table.size, transcendentals=0),
        name="keep",
    )(table)


def fetch_kernel(sectors, heard, occupied, start_label, table, out, row):
    samples = out.shape[0]
    row[...] = jnp.zeros_like(row)
    row[0:1, 0:samples] = start_label[...]
    row[1:2, 0:samples] = occupied[...] * sectors
    label = (jnp.sum(heard[...], axis=0, keepdims=True) + row[0:1, :]) % sectors
    chosen = label + row[1:2, :]
    other = label + sectors - row[1:2, :]
    for s in range(samples):
        out[s, 0] = table[chosen[0, s]].astype(jnp.float32)
        out[s, 1] = table[other[0, s]].astype(jnp.float32)


def times_block(left, block):
    high = left.astype(jnp.bfloat16)
    low = (left - high.astype(jnp.float32)).astype(jnp.bfloat16)
    rows = left.shape[0]
    both = jnp.dot(
        jnp.concatenate([high, low], axis=0), block, preferred_element_type=jnp.float32
    )
    return both[:rows] + both[rows:]


def as_column(row):
    width = row.shape[-1]
    return jnp.broadcast_to(row, (width, width)).T


def products_kernel(group, blocks, start, products, leaving, own_start):
    mine = lax.axis_index("site") % group
    vector = start[pl.ds(mine, 1), :]
    own_start[...] = vector
    left = blocks[0, 0]
    products[0] = left
    for k in range(1, group):
        left = times_block(left, blocks[k, 0].astype(jnp.bfloat16))
        products[k] = left
    leaving[...] = jnp.sum(as_column(vector) * left, axis=0, keepdims=True)


def weights_kernel(sites, group, products, blocks, own_start, arrived, heard, out):
    place, batch = lax.axis_index("site"), lax.axis_index("batch")
    mine, here = place % group, place // group
    groups = sites // group
    vector = jnp.where(here == groups - 1, arrived[...], own_start[...]) if groups > 1 else own_start[...]
    column = as_column(vector)
    rows = [vector]
    for k in range(group):
        rows.append(jnp.sum(column * products[k], axis=0, keepdims=True))
    entering = jnp.concatenate(rows[:group], axis=0)
    after = jnp.concatenate(rows[1:], axis=0)
    columns = entering.T
    beside = []
    for k in range(group):
        column = jnp.broadcast_to(columns[:, k : k + 1], (columns.shape[0],) * 2)
        beside.append(jnp.sum(column * blocks[k, 1], axis=0, keepdims=True))
    beside = jnp.concatenate(beside, axis=0)
    of_chosen = jnp.sum(after * after, axis=1, keepdims=True)
    of_other = jnp.sum(beside * beside, axis=1, keepdims=True)
    notes = heard[pl.ds(pl.multiple_of(batch * sites + here * group, group), group), :]
    occupied = notes[:, group : group + 1]
    total = of_chosen + of_other + epsilon
    fill = jnp.where(occupied == 1, of_chosen, of_other) / total
    log_sum = jnp.sum(jnp.log(of_chosen + epsilon) - jnp.log(total), axis=0, keepdims=True)
    lane = lanes_of((group, LANES))
    fill_own = jnp.where(lane == mine, fill, 0.0)
    fill_cross = jnp.where(lane == 2 * group, fill, 0.0)
    logs = jnp.where(lane == group + mine, log_sum, 0.0)
    for b in range(out.shape[0] // sites):
        for g in range(groups):
            at = b * sites + g * group
            fills = jnp.where(batch == b, fill_own, fill_cross)
            out[at : at + group, :] = jnp.where(here == g, fills, 0.0) + jnp.where(
                batch == b, logs, 0.0
            )


def collect_kernel(sites, batches, reply, fill_probs, mean_logprob, site_fill):
    samples = fill_probs.shape[1]
    row = jnp.sum(reply[...], axis=0, keepdims=True)
    fill_probs[...] = row[:, :samples]
    mean_logprob[...] = row[:, samples : 2 * samples] / sites
    lane = lanes_of(row.shape)
    fills = jnp.where((lane < samples) | (lane == 2 * samples), row, 0.0)
    site_fill[...] = jnp.sum(fills, axis=1, keepdims=True) / (samples * batches)


def call(kernel, out_shape, *arrays, scratch_shapes=(), name=None):
    out_specs = [whole()] * len(out_shape) if isinstance(out_shape, list) else whole()
    return pl.pallas_call(
        kernel,
        in_specs=[whole()] * len(arrays),
        out_specs=out_specs,
        out_shape=out_shape,
        scratch_shapes=scratch_shapes,
        compiler_params=pltpu.CompilerParams(vmem_limit_bytes=VMEM_BYTES),
        name=name,
    )(*arrays)


def on_device(site_tensors, start_vector, start_label, occupations):
    sectors = site_tensors.shape[2]
    width = site_tensors.shape[3]
    sites = lax.axis_size("site")
    batches = lax.axis_size("batch")
    samples = occupations.shape[1]
    group = samples
    groups = sites // group
    everyone = sites * batches
    here = lax.axis_index("site") // group
    f32 = jnp.float32

    table = keep(site_tensors.reshape(2 * sectors, width, width))

    told = call(
        lambda *refs: tell_kernel(sites, group, *refs),
        jax.ShapeDtypeStruct((everyone, LANES), jnp.int32),
        occupations,
        scratch_shapes=[pltpu.VMEM((8, LANES), jnp.int32)],
        name="tell",
    )
    heard = lax.all_to_all(told, ("batch", "site"), 0, 0, tiled=True)

    teams = [[g * group + k for k in range(group)] for g in range(groups)]

    blocks = call(
        lambda *refs: fetch_kernel(sectors, *refs),
        jax.ShapeDtypeStruct((samples, 2, width, width), f32),
        heard,
        occupations,
        start_label[None, :],
        table,
        scratch_shapes=[pltpu.VMEM((8, LANES), jnp.int32)],
        name="fetch",
    )
    blocks = lax.all_to_all(blocks, "site", 0, 0, tiled=True, axis_index_groups=teams)

    row = jax.ShapeDtypeStruct((1, width), f32)
    products, leaving, vector = call(
        lambda *refs: products_kernel(group, *refs),
        [jax.ShapeDtypeStruct((group, width, width), f32), row, row],
        blocks,
        start_vector,
        name="group_products",
    )

    onward = [(i, (i + group) % sites) for i in range(sites)]
    arrived = vector
    for turn in range(1, groups):
        if turn > 1:
            vector = jnp.where(here == turn - 1, arrived, vector)
            leaving = jnp.einsum("sa,ab->sb", vector, products[-1], precision=lax.Precision.HIGHEST)
        arrived = lax.ppermute(leaving, "site", onward)

    message = call(
        lambda *refs: weights_kernel(sites, group, *refs),
        jax.ShapeDtypeStruct((everyone, LANES), f32),
        products,
        blocks,
        vector,
        arrived,
        heard,
        name="group_weights",
    )
    reply = lax.all_to_all(message, ("batch", "site"), 0, 0, tiled=True)
    fill_probs, mean_logprob, site_fill = call(
        lambda *refs: collect_kernel(sites, batches, *refs),
        [
            jax.ShapeDtypeStruct((1, samples), f32),
            jax.ShapeDtypeStruct((1, samples), f32),
            jax.ShapeDtypeStruct((1, 1), f32),
        ],
        reply,
        name="collect",
    )
    return (fill_probs, mean_logprob[0], site_fill[0])


def solution(mesh):
    placed = (P("site", None, None, None, None), P("batch", None), P("batch"), P("site", "batch"))
    return jax.shard_map(
        on_device,
        mesh=mesh,
        in_specs=placed,
        out_specs=(P("site", "batch"), P("batch"), P("site")),
        check_vma=False,
    )
```

time: 250 us -> 50.1 us (0.20)
  waiting for transfers between devices: 109 us -> 9.24 us
  blocking collectives: 116 us -> 26.5 us
  between operations: 15.9 us -> 0.68 us
  starting transfers between devices: 0.04 us -> 7.94 us
  other arithmetic: 4.32 us -> 0 us
  Pallas kernels: 0 us -> 3.22 us
    all_gather x1 -> x0, waiting for transfers between devices: 109 us -> none  [prefix_2(): gathered = lax.all_gather(part, axis)]
    psum x2 -> x0, blocking collectives: 74.2 us -> none  [the longest x1 71.1 us: on_device(): loglik_total = lax.psum(log_term, 'site')]
    all_gather x1 -> x0, blocking collectives: 42.3 us -> none  [prefix_2(): gathered = lax.all_gather(part, axis)]
    all_to_all x0 -> x2, blocking collectives: none -> 26.5 us  [the longest x1 17.7 us: on_device(): lax.all_to_all(blocks, 'site', 0, 0, tiled=True, axis_index_groups=teams)]
    all_to_all x0 -> x1, starting transfers between devices: none -> 7.3 us  [on_device(): heard = lax.all_to_all(told, ('batch', 'site'), 0, 0, tiled=True)]
    all_to_all x0 -> x1, waiting for transfers between devices: none -> 5.37 us  [on_device(): heard = lax.all_to_all(told, ('batch', 'site'), 0, 0, tiled=True)]
    ppermute x0 -> x1, waiting for transfers between devices: none -> 3.87 us  [on_device(): arrived = lax.ppermute(leaving, 'site', onward)]
    pallas_call x0 -> x6, Pallas kernels: none -> 3.22 us  [the longest x5 3.07 us: call(): pl.pallas_call(kernel, in_specs=[whole()] * len(arrays), out_specs=out_sp...]
  transfers between devices with their start and end apart: 1 -> 2, of which waited for: 1 -> 2; matrix products, arithmetic and copies ran while one was open for 0% -> 0% of each run, Pallas kernels for 0% -> 0%
where the time goes in v2:
time: 50.1 us; the launch traced here: 49.8 us
  blocking collectives  26.5 us (53%)
  waiting for transfers between devices  9.24 us (18%)
  starting transfers between devices  7.94 us (16%)
  Pallas kernels  3.22 us (6%)
  local copies, waits for them, and re-layouts  2.25 us (4%)
  between operations  0.68 us (1%)
    all_to_all x1, blocking collectives, on_device(): lax.all_to_all(blocks, 'site', 0, 0, tiled=True, axis_index_groups=teams)  17.7 us
    all_to_all x1, blocking collectives, on_device(): reply = lax.all_to_all(message, ('batch', 'site'), 0, 0, tiled=True)  8.81 us
    all_to_all x1, starting transfers between devices, on_device(): heard = lax.all_to_all(told, ('batch', 'site'), 0, 0, tiled=True)  7.3 us
    all_to_all x1, waiting for transfers between devices, on_device(): heard = lax.all_to_all(told, ('batch', 'site'), 0, 0, tiled=True)  5.37 us
    ppermute x1, waiting for transfers between devices, on_device(): arrived = lax.ppermute(leaving, 'site', onward)  3.87 us
    pallas_call x5, Pallas kernels, call(): pl.pallas_call(kernel, in_specs=[whole()] * len(arrays), out_specs=out_sp...  3.07 us
    unnamed x10, local copies, waits for them, and re-layouts  2.25 us
  transfers between devices with their start and end apart: 2, of which 2 were waited for; matrix products, arithmetic and copies ran while one was open for 0% of the time, Pallas kernels for 0%

profile of v2, /device:TPU:0, one launch (start us, length us, event | category | flops | bytes accessed | tf_op | source)
XLA Modules:
  0.0 49.8 jit_solution(10452588162885752443)
XLA Ops:
  0.6 0.0 copy-start.2
  0.6 0.6 %copy-done.2 = s32[1,8]{1,0:T(1,128)S(1)} copy-done((s32[1,8]{1,0:T(1,128)S(1)}, s32[1,8]{1,0:T(1,128)}, u32[]{:S(2)}) %copy-start.2) | copy-done | bytes 56
  1.3 0.7 %tell.1 = s32[32,128]{1,0:T(8,128)} custom-call(s32[1,8]{1,0:T(1,128)S(1)} %copy-done.2), custom_call_target="tpu_custom_call" | custom-call | tf_op jit(solution)/shard_map/tell/pallas_call | solution.py:149
  2.0 7.3 %all-to-all-start = ((s32[32,1,128]{2,1,0:T(1,128)}), s32[32,1,128]{2,1,0:T(1,128)S(1)}, u32[]{:S(2)}, u32[]{:S(2)}) async-start(s32[32,1,128]{2,1,0:T(1,128)} %bitcast.1), calls=%async_computation | async-start | bytes 32768 | tf_op jit(solution)/shard_map/all_to_all | solution.py:181
  9.3 0.0 copy-start
  9.3 1.6 %copy-done = bf16[1,2,32,128,128]{4,3,2,1,0:T(8,128)(2,1)S(1)} copy-done((bf16[1,2,32,128,128]{4,3,2,1,0:T(8,128)(2,1)S(1)}, bf16[1,2,32,128,128]{4,3,2,1,0:T(8,128)(2,1)}, u32[]{:S(2)}) %copy-start) | copy-done | bytes 2097176
  10.9 0.0 copy-start.3
  10.9 0.0 copy-start.4
  10.9 0.1 keep.1.refs_3_
  11.0 5.4 %all-to-all-done = s32[32,1,128]{2,1,0:T(1,128)S(1)} async-done(((s32[32,1,128]{2,1,0:T(1,128)}), s32[32,1,128]{2,1,0:T(1,128)S(1)}, u32[]{:S(2)}, u32[]{:S(2)}) %all-to-all-start) | async-done | bytes 16416 | tf_op jit(solution)/shard_map/all_to_all | solution.py:181
  16.4 0.0 copy-done.3
  16.4 0.0 copy-done.4
  16.4 0.0 copy-start.1
  16.4 0.2 fetch.1
  16.6 17.7 %all_to_all.27.refs_0_.refs_1_ = f32[8,2,128,128]{3,2,1,0:T(8,128)S(1)} all-to-all(f32[8,2,128,128]{3,2,1,0:T(8,128)S(1)} %fetch.1), channel_id=1, replica_groups={{0,2,4,6,8,10,12,14},{16,18,20,22,24,26,28,30},{1,3,5,7,9,11,13,15},{17..., dimensions={0} | all-to-all | bytes 2097152 | tf_op jit(solution)/shard_map/all_to_all | solution.py:195
  34.3 0.0 copy-done.1
  34.3 1.0 %group_products.1 = (f32[8,128,128]{2,1,0:T(8,128)S(1)}, f32[1,128]{1,0:T(1,128)S(1)}, f32[1,128]{1,0:T(1,128)S(1)}) custom-call(f32[8,2,128,128]{3,2,1,0:T(8,128)S(1)} %all_to_all.27.refs_0_.refs_1_, f32[8,128]{1,0:T(8,128)S(1)} %copy-done.1), custom_call_target="tpu_custom_call" | custom-call | tf_op jit(solution)/shard_map/group_products/pallas_call | solution.py:149
  35.3 0.6 %collective-permute-start = (f32[1,128]{1,0:T(1,128)S(1)}, f32[1,128]{1,0:T(1,128)S(1)}, u32[]{:S(2)}, u32[]{:S(2)}) collective-permute-start(f32[1,128]{1,0:T(1,128)S(1)} %get-tuple-element.11), channel_id=1, source_target_pairs={{0,16},{2,18},{4,20},{6,22},{8,24},{10,26},{12,28},{14,30},{16,0},... | collective-permute-start | bytes 1544 | tf_op jit(solution)/shard_map/ppermute | solution.py:212
  35.9 3.9 %collective-permute-done.refs_3_ = f32[1,128]{1,0:T(1,128)S(1)} collective-permute-done((f32[1,128]{1,0:T(1,128)S(1)}, f32[1,128]{1,0:T(1,128)S(1)}, u32[]{:S(2)}, u32[]{:S(2)}) %collective-permute-start) | collective-permute-done | bytes 544 | tf_op jit(solution)/shard_map/ppermute | solution.py:212
  39.8 0.6 %group_weights.1 = f32[32,128]{1,0:T(8,128)S(1)} custom-call(f32[8,128,128]{2,1,0:T(8,128)S(1)} %get-tuple-element.9.refs_0_, f32[8,2,128,128]{3,2,1,0:T(8,128)S(1)} %all_to_all.27.refs_0_.refs_1_, f32[1,128]{1,0:T(1,128)S(1)} %get-tuple-element.10.refs_2_, f32[1,128]{1,0:T(1,128)S(1)} %collective-permute-done.refs_3_, s32[32,128]{1,0:T(8,128)S(1)} %bitcast.14), custom_call_target="tpu_custom_call" | custom-call | tf_op jit(solution)/shard_map/group_weights/pallas_call | solution.py:149
  40.4 8.8 %all_to_all.28 = f32[32,1,128]{2,1,0:T(1,128)S(1)} all-to-all(f32[32,1,128]{2,1,0:T(1,128)S(1)} %bitcast.15), channel_id=1, replica_groups=mesh['site'=16,'batch'=2] {'batch','site'}, dimensions={0} | all-to-all | bytes 32768 | tf_op jit(solution)/shard_map/all_to_all | solution.py:224
  49.2 0.6 %collect.1 = (f32[1,8]{1,0:T(1,128)}, f32[1,8]{1,0:T(1,128)}, f32[1,1]{1,0:T(1,128)}) custom-call(f32[32,128]{1,0:T(8,128)S(1)} %bitcast.16), custom_call_target="tpu_custom_call" | custom-call | tf_op jit(solution)/shard_map/collect/pallas_call | solution.py:149
Async XLA Ops:
  0.6 0.7 %copy-start.2 = (s32[1,8]{1,0:T(1,128)S(1)}, s32[1,8]{1,0:T(1,128)}, u32[]{:S(2)}) copy-start(s32[1,8]{1,0:T(1,128)} %refs_1_.2) | copy-start | bytes 100
  2.0 14.4 %all-to-all-start = ((s32[32,1,128]{2,1,0:T(1,128)}), s32[32,1,128]{2,1,0:T(1,128)S(1)}, u32[]{:S(2)}, u32[]{:S(2)}) async-start(s32[32,1,128]{2,1,0:T(1,128)} %bitcast.1), calls=%async_computation | async-start | bytes 32768 | tf_op jit(solution)/shard_map/all_to_all | solution.py:181
  9.3 1.6 %copy-start = (bf16[1,2,32,128,128]{4,3,2,1,0:T(8,128)(2,1)S(1)}, bf16[1,2,32,128,128]{4,3,2,1,0:T(8,128)(2,1)}, u32[]{:S(2)}) copy-start(bf16[1,2,32,128,128]{4,3,2,1,0:T(8,128)(2,1)} %param.4) | copy-start | bytes 6291460
  10.9 5.5 %copy-start.3 = (s32[1,8]{1,0:T(1,128)S(1)}, s32[1,8]{1,0:T(1,128)}, u32[]{:S(2)}) copy-start(s32[1,8]{1,0:T(1,128)} %refs_1_.2) | copy-start | bytes 100
  10.9 5.5 %copy-start.4 = (s32[8]{0:T(128)S(1)}, s32[8]{0:T(128)}, u32[]{:S(2)}) copy-start(s32[8]{0:T(128)} %param.6) | copy-start | bytes 100
  16.4 17.9 %copy-start.1 = (f32[8,128]{1,0:T(8,128)S(1)}, f32[8,128]{1,0:T(8,128)}, u32[]{:S(2)}) copy-start(f32[8,128]{1,0:T(8,128)} %refs_1_.3) | copy-start | bytes 12292
  35.3 4.5 %collective-permute-start = (f32[1,128]{1,0:T(1,128)S(1)}, f32[1,128]{1,0:T(1,128)S(1)}, u32[]{:S(2)}, u32[]{:S(2)}) collective-permute-start(f32[1,128]{1,0:T(1,128)S(1)} %get-tuple-element.11), channel_id=1, source_target_pairs={{0,16},{2,18},{4,20},{6,22},{8,24},{10,26},{12,28},{14,30},{16,0},... | collective-permute-start | bytes 1544 | tf_op jit(solution)/shard_map/ppermute | solution.py:212

commit v3 on v2

v3 whole, which is shorter than its diff:
```python
import jax
import jax.numpy as jnp
from jax import lax
from jax.experimental import pallas as pl
from jax.experimental.pallas import tpu as pltpu
from jax.sharding import PartitionSpec as P

epsilon = 1e-06
LANES = 128
VMEM_BYTES = 24 << 20
LEAD = 9
SEATS = (0, 1, 2, 3, 4, 5, 6, 7)


def whole():
    return pl.BlockSpec(memory_space=pltpu.VMEM)


def lanes_of(shape):
    return lax.broadcasted_iota(jnp.int32, shape, 1)


def rows_of(shape):
    return lax.broadcasted_iota(jnp.int32, shape, 0)


def first_order(sites):
    lead = sites * LEAD // 16
    order = list(range(sites))
    order[0], order[lead] = lead, 0
    return order, lead


def swapped(index, lead):
    return jnp.where(index == 0, lead, jnp.where(index == lead, 0, index))


def keep_kernel(table, out, sem):
    copy = pltpu.make_async_copy(table, out, sem)
    copy.start()
    copy.wait()


def keep(table):
    return pl.pallas_call(
        keep_kernel,
        in_specs=[pl.BlockSpec(memory_space=pltpu.HBM)],
        out_specs=whole(),
        scratch_shapes=[pltpu.SemaphoreType.DMA],
        out_shape=jax.ShapeDtypeStruct(table.shape, table.dtype),
        compiler_params=pltpu.CompilerParams(vmem_limit_bytes=VMEM_BYTES),
        cost_estimate=pl.CostEstimate(flops=0, bytes_accessed=4 * table.size, transcendentals=0),
        name="keep",
    )(table)


def fetch_kernel(sectors, seats, lead, heard, occupied, start_label, table, out):
    place = lax.axis_index("site")
    told = heard[:, 0, :]
    earlier = swapped(rows_of(told.shape), lead) < place
    label = jnp.sum(jnp.where(earlier, told, 0), axis=0, keepdims=True) + start_label[...]
    label = label % sectors
    chosen = label + occupied[...] * sectors
    other = label + sectors - occupied[...] * sectors
    for at, s in enumerate(seats):
        out[at, 0] = table[chosen[0, s]].astype(jnp.float32)
        out[at, 1] = table[other[0, s]].astype(jnp.float32)


def halves(x):
    high = x.astype(jnp.bfloat16)
    return high, (x - high.astype(jnp.float32)).astype(jnp.bfloat16)


def times_exact(left, right):
    rows = left.shape[0]
    both = jnp.dot(
        jnp.concatenate(halves(left), axis=0), right, preferred_element_type=jnp.float32
    )
    return both[:rows] + both[rows:]


def times(left, right):
    high, low = halves(right)
    part = jnp.dot(left.astype(jnp.bfloat16), low, preferred_element_type=jnp.float32)
    return times_exact(left, high) + part


def as_column(row):
    width = row.shape[-1]
    return jnp.broadcast_to(row, (width, width)).T


def leaving_kernel(group, seats, blocks, start, leaving, own_start):
    vector = start[pl.ds(lax.axis_index("site") % group, 1), :]
    own_start[...] = vector
    chosen = [blocks[seats.index(k), 0].astype(jnp.bfloat16) for k in range(group)]
    factors = [
        jnp.dot(chosen[k], chosen[k + 1], preferred_element_type=jnp.float32)
        for k in range(0, group - 1, 2)
    ]
    if group % 2:
        factors.append(chosen[-1].astype(jnp.float32))
    while len(factors) > 2:
        tail = factors[len(factors) // 2 * 2 :]
        factors = [times(factors[k], factors[k + 1]) for k in range(0, len(factors) - 1, 2)] + tail
    for factor in factors:
        vector = jnp.sum(as_column(vector) * factor, axis=0, keepdims=True)
    leaving[...] = vector


def products_kernel(group, seats, blocks, products):
    for k in range(group):
        chosen, other = blocks[seats.index(k), 0], blocks[seats.index(k), 1]
        if k == 0:
            left, beside = chosen, other
        else:
            beside = times_exact(left, other.astype(jnp.bfloat16))
            left = times_exact(left, chosen.astype(jnp.bfloat16))
        products[0, k] = left
        products[1, k] = beside


def weights_kernel(sites, group, lead, products, own_start, arrived, heard, out):
    place, batch = lax.axis_index("site"), lax.axis_index("batch")
    mine, here = place % group, place // group
    groups = sites // group
    vector = own_start[...]
    if groups > 1:
        vector = jnp.where(here == groups - 1, arrived[...], vector)
    column = as_column(vector)

    def weight(n):
        rows = [jnp.sum(column * products[n, k], axis=0, keepdims=True) for k in range(group)]
        rows = jnp.concatenate(rows, axis=0)
        return jnp.sum(rows * rows, axis=1, keepdims=True)

    of_chosen, of_other = weight(0), weight(1)
    notes = jnp.concatenate(
        [heard[swapped(here * group + k, lead)] for k in range(group)], axis=0
    )
    notes = jnp.where(lanes_of(notes.shape) == mine, notes, 0)
    occupied = jnp.sum(notes, axis=1, keepdims=True)
    total = of_chosen + of_other + epsilon
    fill = jnp.where(occupied == 1, of_chosen, of_other) / total
    log_sum = jnp.sum(jnp.log(of_chosen + epsilon) - jnp.log(total), axis=0, keepdims=True)
    lane = lanes_of((group, LANES))
    fill_own = jnp.where(lane == mine, fill, 0.0)
    fill_cross = jnp.where(lane == 2 * group, fill, 0.0)
    logs = jnp.where(lane == group + mine, log_sum, 0.0)
    for b in range(out.shape[0] // sites):
        for g in range(groups):
            at = b * sites + g * group
            fills = jnp.where(batch == b, fill_own, fill_cross)
            out[at : at + group, :] = jnp.where(here == g, fills, 0.0) + jnp.where(
                batch == b, logs, 0.0
            )


def collect_kernel(sites, batches, reply, fill_probs, mean_logprob, site_fill):
    samples = fill_probs.shape[1]
    row = jnp.sum(reply[...], axis=0, keepdims=True)
    fill_probs[...] = row[:, :samples]
    mean_logprob[...] = row[:, samples : 2 * samples] / sites
    lane = lanes_of(row.shape)
    fills = jnp.where((lane < samples) | (lane == 2 * samples), row, 0.0)
    site_fill[...] = jnp.sum(fills, axis=1, keepdims=True) / (samples * batches)


def call(kernel, out_shape, *arrays, scratch_shapes=(), name=None):
    out_specs = [whole()] * len(out_shape) if isinstance(out_shape, list) else whole()
    return pl.pallas_call(
        kernel,
        in_specs=[whole()] * len(arrays),
        out_specs=out_specs,
        out_shape=out_shape,
        scratch_shapes=scratch_shapes,
        compiler_params=pltpu.CompilerParams(vmem_limit_bytes=VMEM_BYTES),
        name=name,
    )(*arrays)


def on_device(site_tensors, start_vector, start_label, occupations):
    sectors = site_tensors.shape[2]
    width = site_tensors.shape[3]
    sites = lax.axis_size("site")
    batches = lax.axis_size("batch")
    samples = occupations.shape[1]
    group = samples
    groups = sites // group
    everyone = sites * batches
    here = lax.axis_index("site") // group
    f32 = jnp.float32

    table = keep(site_tensors.reshape(2 * sectors, width, width))

    order, lead = first_order(sites)
    told = jnp.broadcast_to(occupations[:, None, :], (sites, 1, samples))
    heard = lax.all_to_all(told, "site", 0, 0, tiled=True, axis_index_groups=[order])

    seats = SEATS if group == len(SEATS) else tuple(range(group))
    teams = [[g * group + k for k in seats] for g in range(groups)]

    blocks = call(
        lambda *refs: fetch_kernel(sectors, seats, lead, *refs),
        jax.ShapeDtypeStruct((samples, 2, width, width), f32),
        heard,
        occupations,
        start_label[None, :],
        table,
        name="fetch",
    )
    blocks = lax.all_to_all(blocks, "site", 0, 0, tiled=True, axis_index_groups=teams)

    row = jax.ShapeDtypeStruct((1, width), f32)
    leaving, vector = call(
        lambda *refs: leaving_kernel(group, seats, *refs),
        [row, row],
        blocks,
        start_vector,
        name="leaving",
    )
    products = call(
        lambda *refs: products_kernel(group, seats, *refs),
        jax.ShapeDtypeStruct((2, group, width, width), f32),
        blocks,
        name="products",
    )

    onward = [(i, (i + group) % sites) for i in range(sites)]
    arrived = vector
    for turn in range(1, groups):
        if turn > 1:
            vector = jnp.where(here == turn - 1, arrived, vector)
            leaving = jnp.einsum("sa,ab->sb", vector, products[0, -1], precision=lax.Precision.HIGHEST)
        arrived = lax.ppermute(leaving, "site", onward)

    message = call(
        lambda *refs: weights_kernel(sites, group, lead, *refs),
        jax.ShapeDtypeStruct((everyone, LANES), f32),
        products,
        vector,
        arrived,
        heard,
        name="group_weights",
    )
    reply = lax.all_to_all(message, ("batch", "site"), 0, 0, tiled=True)
    fill_probs, mean_logprob, site_fill = call(
        lambda *refs: collect_kernel(sites, batches, *refs),
        [
            jax.ShapeDtypeStruct((1, samples), f32),
            jax.ShapeDtypeStruct((1, samples), f32),
            jax.ShapeDtypeStruct((1, 1), f32),
        ],
        reply,
        name="collect",
    )
    return (fill_probs, mean_logprob[0], site_fill[0])


def solution(mesh):
    placed = (P("site", None, None, None, None), P("batch", None), P("batch"), P("site", "batch"))
    return jax.shard_map(
        on_device,
        mesh=mesh,
        in_specs=placed,
        out_specs=(P("site", "batch"), P("batch"), P("site")),
        check_vma=False,
    )
```

time: 50.1 us -> 47.3 us (0.944)
  waiting for transfers between devices: 9.24 us -> 3.59 us
  starting transfers between devices: 7.94 us -> 11 us
  local copies, waits for them, and re-layouts: 2.25 us -> 2.85 us
  Pallas kernels: 3.22 us -> 2.69 us
    all_to_all x1, waiting for transfers between devices: 5.37 us -> 2.38 us  [on_device(): lax.all_to_all(told, 'site', 0, 0, tiled=True, axis_index_groups=[order])]
    ppermute x1, waiting for transfers between devices: 3.87 us -> 1.21 us  [on_device(): arrived = lax.ppermute(leaving, 'site', onward)]
    ppermute x1, starting transfers between devices: 0.64 us -> 2.26 us  [on_device(): arrived = lax.ppermute(leaving, 'site', onward)]
    all_to_all x1, starting transfers between devices: 7.3 us -> 8.79 us  [on_device(): lax.all_to_all(told, 'site', 0, 0, tiled=True, axis_index_groups=[order])]
    all_to_all x1, blocking collectives: 17.7 us -> 16.3 us  [on_device(): lax.all_to_all(blocks, 'site', 0, 0, tiled=True, axis_index_groups=teams)]
    broadcast_in_dim x0 -> x1, local copies, waits for them, and re-layouts: none -> 1.26 us  [on_device(): told = jnp.broadcast_to(occupations[:, None, :], (sites, 1, samples))]
    all_to_all x1, blocking collectives: 8.81 us -> 9.85 us  [on_device(): reply = lax.all_to_all(message, ('batch', 'site'), 0, 0, tiled=True)]
    unnamed x10 -> x8, local copies, waits for them, and re-layouts: 2.25 us -> 1.6 us
  transfers between devices with their start and end apart: 2 -> 2, of which waited for: 2 -> 2; matrix products, arithmetic and copies ran while one was open for 0% -> 0% of each run, Pallas kernels for 0% -> 3%
where the time goes in v3:
time: 47.3 us; the launch traced here: 47 us
  blocking collectives  26.2 us (55%)
  starting transfers between devices  11 us (23%)
  waiting for transfers between devices  3.59 us (8%)
  local copies, waits for them, and re-layouts  2.85 us (6%)
  Pallas kernels  2.69 us (6%)
  between operations  0.68 us (1%)
    all_to_all x1, blocking collectives, on_device(): lax.all_to_all(blocks, 'site', 0, 0, tiled=True, axis_index_groups=teams)  16.3 us
    all_to_all x1, blocking collectives, on_device(): reply = lax.all_to_all(message, ('batch', 'site'), 0, 0, tiled=True)  9.85 us
    all_to_all x1, starting transfers between devices, on_device(): lax.all_to_all(told, 'site', 0, 0, tiled=True, axis_index_groups=[order])  8.79 us
    pallas_call x5, Pallas kernels, call(): pl.pallas_call(kernel, in_specs=[whole()] * len(arrays), out_specs=out_sp...  2.54 us
    all_to_all x1, waiting for transfers between devices, on_device(): lax.all_to_all(told, 'site', 0, 0, tiled=True, axis_index_groups=[order])  2.38 us
    ppermute x1, starting transfers between devices, on_device(): arrived = lax.ppermute(leaving, 'site', onward)  2.26 us
    unnamed x8, local copies, waits for them, and re-layouts  1.6 us
    broadcast_in_dim x1, local copies, waits for them, and re-layouts, on_device(): told = jnp.broadcast_to(occupations[:, None, :], (sites, 1, samples))  1.26 us
  transfers between devices with their start and end apart: 2, of which 2 were waited for; matrix products, arithmetic and copies ran while one was open for 0% of the time, Pallas kernels for 3%

profile of v3, /device:TPU:0, one launch (start us, length us, event | category | flops | bytes accessed | tf_op | source)
XLA Modules:
  0.0 47.0 jit_solution(14980395175978055652)
XLA Ops:
  0.6 1.3 %broadcast_in_dim.12 = s32[16,1,8]{2,1,0:T(1,128)} broadcast(s32[8]{0:T(128)} %bitcast.12), dimensions={2} | broadcast | bytes 544 | tf_op jit(solution)/shard_map/broadcast_in_dim | solution.py:198
  1.9 8.8 %all-to-all-start = ((s32[16,1,8]{2,1,0:T(1,128)}), s32[16,1,8]{2,1,0:T(1,128)S(1)}, u32[]{:S(2)}, u32[]{:S(2)}) async-start(s32[16,1,8]{2,1,0:T(1,128)} %broadcast_in_dim.12), calls=%async_computation | async-start | bytes 16384 | tf_op jit(solution)/shard_map/all_to_all | solution.py:199
  10.7 0.0 copy-start
  10.7 1.6 %copy-done = bf16[1,2,32,128,128]{4,3,2,1,0:T(8,128)(2,1)S(1)} copy-done((bf16[1,2,32,128,128]{4,3,2,1,0:T(8,128)(2,1)S(1)}, bf16[1,2,32,128,128]{4,3,2,1,0:T(8,128)(2,1)}, u32[]{:S(2)}) %copy-start) | copy-done | bytes 2097176
  12.3 0.0 copy-start.2
  12.3 0.0 copy-start.3
  12.3 0.1 keep.1.refs_3_
  12.4 2.4 %all-to-all-done.refs_0_.refs_3_ = s32[16,1,8]{2,1,0:T(1,128)S(1)} async-done(((s32[16,1,8]{2,1,0:T(1,128)}), s32[16,1,8]{2,1,0:T(1,128)S(1)}, u32[]{:S(2)}, u32[]{:S(2)}) %all-to-all-start) | async-done | bytes 544 | tf_op jit(solution)/shard_map/all_to_all | solution.py:199
  14.8 0.0 copy-done.2
  14.8 0.0 copy-done.3
  14.8 0.0 copy-start.1
  14.8 0.2 fetch.1
  15.0 16.3 %all_to_all.21.refs_0_ = f32[8,2,128,128]{3,2,1,0:T(8,128)S(1)} all-to-all(f32[8,2,128,128]{3,2,1,0:T(8,128)S(1)} %fetch.1), channel_id=1, replica_groups={{0,2,4,6,8,10,12,14},{16,18,20,22,24,26,28,30},{1,3,5,7,9,11,13,15},{17..., dimensions={0} | all-to-all | bytes 2097152 | tf_op jit(solution)/shard_map/all_to_all | solution.py:213
  31.3 0.0 copy-done.1
  31.3 0.4 leaving.1
  31.8 2.3 %collective-permute-start = (f32[1,128]{1,0:T(1,128)S(1)}, f32[1,128]{1,0:T(1,128)S(1)}, u32[]{:S(2)}, u32[]{:S(2)}) collective-permute-start(f32[1,128]{1,0:T(1,128)S(1)} %get-tuple-element.9), channel_id=1, source_target_pairs={{0,16},{2,18},{4,20},{6,22},{8,24},{10,26},{12,28},{14,30},{16,0},... | collective-permute-start | bytes 1544 | tf_op jit(solution)/shard_map/ppermute | solution.py:236
  34.0 1.0 %products.1.refs_0_ = f32[2,8,128,128]{3,2,1,0:T(8,128)S(1)} custom-call(f32[8,2,128,128]{3,2,1,0:T(8,128)S(1)} %all_to_all.21.refs_0_), custom_call_target="tpu_custom_call" | custom-call | tf_op jit(solution)/shard_map/products/pallas_call | solution.py:172
  35.1 1.2 %collective-permute-done.refs_2_ = f32[1,128]{1,0:T(1,128)S(1)} collective-permute-done((f32[1,128]{1,0:T(1,128)S(1)}, f32[1,128]{1,0:T(1,128)S(1)}, u32[]{:S(2)}, u32[]{:S(2)}) %collective-permute-start) | collective-permute-done | bytes 544 | tf_op jit(solution)/shard_map/ppermute | solution.py:236
  36.3 0.3 group_weights.1
  36.6 9.9 %all_to_all.22 = f32[32,1,128]{2,1,0:T(1,128)S(1)} all-to-all(f32[32,1,128]{2,1,0:T(1,128)S(1)} %bitcast.10), channel_id=1, replica_groups=mesh['site'=16,'batch'=2] {'batch','site'}, dimensions={0} | all-to-all | bytes 32768 | tf_op jit(solution)/shard_map/all_to_all | solution.py:247
  46.4 0.6 %collect.1 = (f32[1,8]{1,0:T(1,128)}, f32[1,8]{1,0:T(1,128)}, f32[1,1]{1,0:T(1,128)}) custom-call(f32[32,128]{1,0:T(8,128)S(1)} %bitcast.11), custom_call_target="tpu_custom_call" | custom-call | tf_op jit(solution)/shard_map/collect/pallas_call | solution.py:172
Async XLA Ops:
  1.9 12.9 %all-to-all-start = ((s32[16,1,8]{2,1,0:T(1,128)}), s32[16,1,8]{2,1,0:T(1,128)S(1)}, u32[]{:S(2)}, u32[]{:S(2)}) async-start(s32[16,1,8]{2,1,0:T(1,128)} %broadcast_in_dim.12), calls=%async_computation | async-start | bytes 16384 | tf_op jit(solution)/shard_map/all_to_all | solution.py:199
  10.7 1.6 %copy-start = (bf16[1,2,32,128,128]{4,3,2,1,0:T(8,128)(2,1)S(1)}, bf16[1,2,32,128,128]{4,3,2,1,0:T(8,128)(2,1)}, u32[]{:S(2)}) copy-start(bf16[1,2,32,128,128]{4,3,2,1,0:T(8,128)(2,1)} %param.4) | copy-start | bytes 6291460
  12.3 2.5 %copy-start.2 = (s32[1,8]{1,0:T(1,128)S(1)}, s32[1,8]{1,0:T(1,128)}, u32[]{:S(2)}) copy-start(s32[1,8]{1,0:T(1,128)} %refs_1_.2) | copy-start | bytes 100
  12.3 2.5 %copy-start.3 = (s32[8]{0:T(128)S(1)}, s32[8]{0:T(128)}, u32[]{:S(2)}) copy-start(s32[8]{0:T(128)} %param.6) | copy-start | bytes 100
  14.8 16.5 %copy-start.1 = (f32[8,128]{1,0:T(8,128)S(1)}, f32[8,128]{1,0:T(8,128)}, u32[]{:S(2)}) copy-start(f32[8,128]{1,0:T(8,128)} %refs_1_.3) | copy-start | bytes 12292
  31.8 4.5 %collective-permute-start = (f32[1,128]{1,0:T(1,128)S(1)}, f32[1,128]{1,0:T(1,128)S(1)}, u32[]{:S(2)}, u32[]{:S(2)}) collective-permute-start(f32[1,128]{1,0:T(1,128)S(1)} %get-tuple-element.9), channel_id=1, source_target_pairs={{0,16},{2,18},{4,20},{6,22},{8,24},{10,26},{12,28},{14,30},{16,0},... | collective-permute-start | bytes 1544 | tf_op jit(solution)/shard_map/ppermute | solution.py:236

commit v4 on v3

v4 whole, which is shorter than its diff:
```python
import jax
import jax.numpy as jnp
from jax import lax
from jax.experimental import pallas as pl
from jax.experimental.pallas import tpu as pltpu
from jax.sharding import PartitionSpec as P

epsilon = 1e-06
LANES = 128
VMEM_BYTES = 24 << 20
LEAD = 9


def whole():
    return pl.BlockSpec(memory_space=pltpu.VMEM)


def lanes_of(shape):
    return lax.broadcasted_iota(jnp.int32, shape, 1)


def rows_of(shape):
    return lax.broadcasted_iota(jnp.int32, shape, 0)


def first_order(sites):
    lead = sites * LEAD // 16
    order = list(range(sites))
    order[0], order[lead] = lead, 0
    return order, lead


def swapped(index, lead):
    return jnp.where(index == 0, lead, jnp.where(index == lead, 0, index))


def keep_kernel(table, out, sem):
    copy = pltpu.make_async_copy(table, out, sem)
    copy.start()
    copy.wait()


def keep(table):
    return pl.pallas_call(
        keep_kernel,
        in_specs=[pl.BlockSpec(memory_space=pltpu.HBM)],
        out_specs=whole(),
        scratch_shapes=[pltpu.SemaphoreType.DMA],
        out_shape=jax.ShapeDtypeStruct(table.shape, table.dtype),
        compiler_params=pltpu.CompilerParams(vmem_limit_bytes=VMEM_BYTES),
        cost_estimate=pl.CostEstimate(flops=0, bytes_accessed=4 * table.size, transcendentals=0),
        name="keep",
    )(table)


def picks_of(sectors, lead, heard, occupied, start_label):
    place = lax.axis_index("site")
    told = heard[:, 0, :]
    earlier = swapped(rows_of(told.shape), lead) < place
    label = jnp.sum(jnp.where(earlier, told, 0), axis=0, keepdims=True) + start_label[...]
    label = label % sectors
    chosen = label + occupied[...] * sectors
    return chosen, label + sectors - occupied[...] * sectors


def fetch_kernel(sectors, lead, heard, occupied, start_label, table, out):
    picks = picks_of(sectors, lead, heard, occupied, start_label)
    for s in range(out.shape[0]):
        for n in range(out.shape[1]):
            out[s, n] = table[picks[n][0, s]].astype(jnp.float32)


def halves(x):
    high = x.astype(jnp.bfloat16)
    return high, (x - high.astype(jnp.float32)).astype(jnp.bfloat16)


def times_exact(left, right):
    rows = left.shape[0]
    both = jnp.dot(
        jnp.concatenate(halves(left), axis=0), right, preferred_element_type=jnp.float32
    )
    return both[:rows] + both[rows:]


def times(left, right):
    high, low = halves(right)
    part = jnp.dot(left.astype(jnp.bfloat16), low, preferred_element_type=jnp.float32)
    return times_exact(left, high) + part


def as_column(row):
    width = row.shape[-1]
    return jnp.broadcast_to(row, (width, width)).T


def row_times(row, block):
    return jnp.sum(as_column(row) * block, axis=0, keepdims=True)


def vectors(blocks, vector, group):
    entering = [vector]
    chosen = [blocks[k, 0].astype(jnp.bfloat16) for k in range(group)]
    for k in range(0, group - 3, 4):
        one, two = (
            jnp.dot(chosen[j], chosen[j + 1], preferred_element_type=jnp.float32)
            for j in (k, k + 2)
        )
        vector = entering[-1]
        middle = row_times(vector, one)
        entering += [
            row_times(vector, blocks[k, 0]),
            middle,
            row_times(middle, blocks[k + 2, 0]),
            row_times(vector, times(one, two)),
        ]
    while len(entering) <= group:
        entering.append(row_times(entering[-1], blocks[len(entering) - 1, 0]))
    return entering


def first_kernel(group, blocks, start, entering, leaving):
    vector = start[pl.ds(lax.axis_index("site") % group, 1), :]
    found = vectors(blocks, vector, group)
    leaving[...] = found[-1]
    for k in range(group):
        entering[k] = found[k]


def products_kernel(group, blocks, product):
    left = blocks[0, 0]
    for k in range(1, group):
        left = times_exact(left, blocks[k, 0].astype(jnp.bfloat16))
    product[...] = left


def shares(of_chosen, of_other, occupied):
    total = of_chosen + of_other + epsilon
    fill = jnp.where(occupied == 1, of_chosen, of_other) / total
    return fill, jnp.log(of_chosen + epsilon) - jnp.log(total)


def squares(row):
    return jnp.sum(row * row, axis=1, keepdims=True)


def site_kernel(sectors, sites, lead, returned, heard, occupied, start_label, table, out):
    place, batch = lax.axis_index("site"), lax.axis_index("batch")
    picks = picks_of(sectors, lead, heard, occupied, start_label)
    samples = returned.shape[0]
    found = [[], []]
    for s in range(samples):
        column = as_column(returned[s])
        for n in range(2):
            block = table[picks[n][0, s]].astype(jnp.float32)
            found[n].append(jnp.sum(column * block, axis=0, keepdims=True))
    of_chosen, of_other = (squares(jnp.concatenate(rows, axis=0)) for rows in found)
    own = (samples, samples)
    mark = jnp.where(lanes_of(own) == rows_of(own), jnp.broadcast_to(occupied[...], own), 0)
    fill, log = shares(of_chosen, of_other, jnp.sum(mark, axis=1, keepdims=True))
    shape = (samples, LANES)
    lane, row = lanes_of(shape), rows_of(shape)
    logs = jnp.sum(jnp.where(lane == row + samples, log, 0.0), axis=0, keepdims=True)
    fills = jnp.sum(jnp.where(lane == row, fill, 0.0), axis=0, keepdims=True)
    cross = jnp.sum(jnp.where(lane == 2 * samples, fill, 0.0), axis=0, keepdims=True)
    to = rows_of(out.shape)
    here, own = to % sites == place, to // sites == batch
    out[...] = jnp.where(own, logs, 0.0) + jnp.where(here, jnp.where(own, fills, cross), 0.0)


def weights_kernel(sites, group, lead, from_site, blocks, arrived, heard, out):
    place, batch = lax.axis_index("site"), lax.axis_index("batch")
    mine, here = place % group, place // group
    groups = sites // group

    @pl.when(here == 0)
    def _():
        out[...] = from_site[...]

    @pl.when(here > 0)
    def _():
        entering = vectors(blocks, arrived[...], group)
        of_chosen = squares(jnp.concatenate(entering[1:], axis=0))
        beside = [row_times(entering[k], blocks[k, 1]) for k in range(group)]
        of_other = squares(jnp.concatenate(beside, axis=0))
        notes = jnp.concatenate(
            [heard[swapped(here * group + k, lead)] for k in range(group)], axis=0
        )
        notes = jnp.where(lanes_of(notes.shape) == mine, notes, 0)
        fill, log = shares(of_chosen, of_other, jnp.sum(notes, axis=1, keepdims=True))
        lane = lanes_of((group, LANES))
        fill_own = jnp.where(lane == mine, fill, 0.0)
        fill_cross = jnp.where(lane == 2 * group, fill, 0.0)
        log_sum = jnp.sum(log, axis=0, keepdims=True)
        logs = jnp.where(lane == group + mine, log_sum, 0.0)
        for b in range(out.shape[0] // sites):
            for g in range(groups):
                at = b * sites + g * group
                fills = jnp.where(batch == b, fill_own, fill_cross)
                out[at : at + group, :] = jnp.where(here == g, fills, 0.0) + jnp.where(
                    batch == b, logs, 0.0
                )


def collect_kernel(sites, batches, reply, fill_probs, mean_logprob, site_fill):
    samples = fill_probs.shape[1]
    row = jnp.sum(reply[...], axis=0, keepdims=True)
    fill_probs[...] = row[:, :samples]
    mean_logprob[...] = row[:, samples : 2 * samples] / sites
    lane = lanes_of(row.shape)
    fills = jnp.where((lane < samples) | (lane == 2 * samples), row, 0.0)
    site_fill[...] = jnp.sum(fills, axis=1, keepdims=True) / (samples * batches)


def call(kernel, out_shape, *arrays, scratch_shapes=(), name=None):
    out_specs = [whole()] * len(out_shape) if isinstance(out_shape, (list, tuple)) else whole()
    return pl.pallas_call(
        kernel,
        in_specs=[whole()] * len(arrays),
        out_specs=out_specs,
        out_shape=out_shape,
        scratch_shapes=scratch_shapes,
        compiler_params=pltpu.CompilerParams(vmem_limit_bytes=VMEM_BYTES),
        name=name,
    )(*arrays)


def on_device(site_tensors, start_vector, start_label, occupations):
    sectors = site_tensors.shape[2]
    width = site_tensors.shape[3]
    sites = lax.axis_size("site")
    batches = lax.axis_size("batch")
    samples = occupations.shape[1]
    group = samples
    groups = sites // group
    everyone = sites * batches
    here = lax.axis_index("site") // group
    f32 = jnp.float32

    table = keep(site_tensors.reshape(2 * sectors, width, width))

    order, lead = first_order(sites)
    told = jnp.broadcast_to(occupations[:, None, :], (sites, 1, samples))
    heard = lax.all_to_all(told, "site", 0, 0, tiled=True, axis_index_groups=[order])

    teams = [[g * group + k for k in range(group)] for g in range(groups)]
    given = (heard, occupations, start_label[None, :], table)
    message_like = jax.ShapeDtypeStruct((everyone, LANES), f32)

    def trade(blocks):
        return lax.all_to_all(blocks, "site", 0, 0, tiled=True, axis_index_groups=teams)

    def fetch(count):
        return call(
            lambda *refs: fetch_kernel(sectors, lead, *refs),
            jax.ShapeDtypeStruct((samples, count, width, width), f32),
            *given,
            name="fetch",
        )

    def first():
        return call(
            lambda *refs: first_kernel(group, *refs),
            (
                jax.ShapeDtypeStruct((group, 1, width), f32),
                jax.ShapeDtypeStruct((1, width), f32),
            ),
            trade(fetch(1)),
            start_vector,
            name="first",
        )

    def first_idle():
        return jnp.zeros((group, 1, width), f32), jnp.zeros((1, width), f32)

    def second(entering):
        message = call(
            lambda *refs: site_kernel(sectors, sites, lead, *refs),
            message_like,
            trade(entering),
            *given,
            name="site_weights",
        )
        return message, jnp.zeros((group, 2, width, width), f32)

    def later(entering):
        return jnp.zeros(message_like.shape, f32), trade(fetch(2))

    entering, leaving = lax.cond(here == 0, first, first_idle)
    vector = leaving
    if groups > 1:
        onward = [(i, i + group) for i in range(group)]
        vector = lax.ppermute(leaving, "site", onward)
    from_site, blocks = lax.cond(here == 0, second, later, entering)
    if groups > 2:
        product = call(
            lambda *refs: products_kernel(group, *refs),
            jax.ShapeDtypeStruct((width, width), f32),
            blocks,
            name="product",
        )
    for turn in range(2, groups):
        leaving = jnp.dot(vector, product, precision=lax.Precision.HIGHEST)
        onward = [(i, i + group) for i in range((turn - 1) * group, turn * group)]
        arrived = lax.ppermute(leaving, "site", onward)
        vector = jnp.where(here == turn, arrived, vector)

    message = call(
        lambda *refs: weights_kernel(sites, group, lead, *refs),
        message_like,
        from_site,
        blocks,
        vector,
        heard,
        name="group_weights",
    )
    reply = lax.all_to_all(message, ("batch", "site"), 0, 0, tiled=True)
    fill_probs, mean_logprob, site_fill = call(
        lambda *refs: collect_kernel(sites, batches, *refs),
        [
            jax.ShapeDtypeStruct((1, samples), f32),
            jax.ShapeDtypeStruct((1, samples), f32),
            jax.ShapeDtypeStruct((1, 1), f32),
        ],
        reply,
        name="collect",
    )
    return (fill_probs, mean_logprob[0], site_fill[0])


def solution(mesh):
    placed = (P("site", None, None, None, None), P("batch", None), P("batch"), P("site", "batch"))
    return jax.shard_map(
        on_device,
        mesh=mesh,
        in_specs=placed,
        out_specs=(P("site", "batch"), P("batch"), P("site")),
        check_vma=False,
    )
```

time: 47.3 us -> 45.8 us (0.968)
  waiting for transfers between devices: 3.59 us -> 2.36 us
  blocking collectives: 26.2 us -> 27.4 us
  starting transfers between devices: 11 us -> 10.1 us
  Pallas kernels: 2.69 us -> 1.9 us
    all_to_all x1 -> x2, blocking collectives: 16.3 us -> 18.6 us  [trade(): lax.all_to_all(blocks, 'site', 0, 0, tiled=True, axis_index_groups=teams)]
    ppermute x1, waiting for transfers between devices: 1.21 us -> 0.01 us  [on_device(): vector = lax.ppermute(leaving, 'site', onward)]
    all_to_all x1, blocking collectives: 9.85 us -> 8.82 us  [on_device(): reply = lax.all_to_all(message, ('batch', 'site'), 0, 0, tiled=True)]
    ppermute x1, starting transfers between devices: 2.26 us -> 1.29 us  [on_device(): vector = lax.ppermute(leaving, 'site', onward)]
    pallas_call x5, Pallas kernels: 2.54 us -> 1.75 us  [call(): pl.pallas_call(kernel, in_specs=[whole()] * len(arrays), out_specs=out_sp...]
  transfers between devices with their start and end apart: 2 -> 2, of which waited for: 2 -> 1; matrix products, arithmetic and copies ran while one was open for 0% -> 0% of each run, Pallas kernels for 3% -> 1%
where the time goes in v4:
time: 45.8 us; the launch traced here: 45.5 us
  blocking collectives  27.4 us (60%)
  starting transfers between devices  10.1 us (22%)
  local copies, waits for them, and re-layouts  2.95 us (6%)
  waiting for transfers between devices  2.36 us (5%)
  Pallas kernels  1.9 us (4%)
  between operations  0.69 us (2%)
    all_to_all x2, blocking collectives, trade(): lax.all_to_all(blocks, 'site', 0, 0, tiled=True, axis_index_groups=teams)  18.6 us
    all_to_all x1, blocking collectives, on_device(): reply = lax.all_to_all(message, ('batch', 'site'), 0, 0, tiled=True)  8.82 us
    all_to_all x1, starting transfers between devices, on_device(): lax.all_to_all(told, 'site', 0, 0, tiled=True, axis_index_groups=[order])  8.79 us
    all_to_all x1, waiting for transfers between devices, on_device(): lax.all_to_all(told, 'site', 0, 0, tiled=True, axis_index_groups=[order])  2.35 us
    pallas_call x5, Pallas kernels, call(): pl.pallas_call(kernel, in_specs=[whole()] * len(arrays), out_specs=out_sp...  1.75 us
    unnamed x8, local copies, waits for them, and re-layouts  1.6 us
    ppermute x1, starting transfers between devices, on_device(): vector = lax.ppermute(leaving, 'site', onward)  1.29 us
    broadcast_in_dim x1, local copies, waits for them, and re-layouts, on_device(): told = jnp.broadcast_to(occupations[:, None, :], (sites, 1, samples))  1.26 us
  transfers between devices with their start and end apart: 2, of which 1 were waited for; matrix products, arithmetic and copies ran while one was open for 0% of the time, Pallas kernels for 1%

profile of v4, /device:TPU:0, one launch (start us, length us, event | category | flops | bytes accessed | tf_op | source)
XLA Modules:
  0.0 45.5 jit_solution(7378504164378842738)
XLA Ops:
  0.6 1.3 %broadcast_in_dim.12 = s32[16,1,8]{2,1,0:T(1,128)} broadcast(s32[8]{0:T(128)} %bitcast.12), dimensions={2} | broadcast | bytes 544 | tf_op jit(solution)/shard_map/broadcast_in_dim | solution.py:243
  1.9 8.8 %all-to-all-start.3 = ((s32[16,1,8]{2,1,0:T(1,128)}), s32[16,1,8]{2,1,0:T(1,128)S(1)}, u32[]{:S(2)}, u32[]{:S(2)}) async-start(s32[16,1,8]{2,1,0:T(1,128)} %broadcast_in_dim.12), calls=%async_computation.3 | async-start | bytes 16384 | tf_op jit(solution)/shard_map/all_to_all | solution.py:244
  10.7 0.0 copy-start
  10.7 1.6 %copy-done = bf16[1,2,32,128,128]{4,3,2,1,0:T(8,128)(2,1)S(1)} copy-done((bf16[1,2,32,128,128]{4,3,2,1,0:T(8,128)(2,1)S(1)}, bf16[1,2,32,128,128]{4,3,2,1,0:T(8,128)(2,1)}, u32[]{:S(2)}) %copy-start) | copy-done | bytes 2097176
  12.3 0.0 copy-start.1
  12.3 0.0 copy-start.2
  12.3 0.0 copy-start.3
  12.3 0.1 keep.1
  12.4 2.4 %all-to-all-done.3.refs_3_ = s32[16,1,8]{2,1,0:T(1,128)S(1)} async-done(((s32[16,1,8]{2,1,0:T(1,128)}), s32[16,1,8]{2,1,0:T(1,128)S(1)}, u32[]{:S(2)}, u32[]{:S(2)}) %all-to-all-start.3) | async-done | bytes 544 | tf_op jit(solution)/shard_map/all_to_all | solution.py:244
  14.8 0.0 copy-done.1
  14.8 0.0 copy-done.2
  14.8 0.0 copy-done.3
  14.8 11.5 %conditional.2 = ((f32[8,1,128]{2,1,0:T(1,128)S(1)}, f32[1,128]{1,0:T(1,128)S(1)})) conditional(s32[]{:T(128)} %convert_element_type.4, () %tuple.24, (s32[16,1,8]{2,1,0:T(1,128)S(1)}, s32[1,8]{1,0:T(1,128)S(1)}, s32[1,8]{1,0:T(1,128)S(1)}, bf16[64,128,128]{2,1,0:T(8,128)(2,1)S(1)}, f32[8,128]{1,0:T(8,128)S(1)}) %tuple.40), branch_computations={%region_0.1_spmd, %region_1.2_spmd} | conditional | bytes 1048584 | solution.py:289
  14.8 0.2 fetch.2
  15.0 10.7 %all_to_all.28.refs_0_ = f32[8,1,128,128]{3,2,1,0:T(8,128)S(1)} all-to-all(f32[8,1,128,128]{3,2,1,0:T(8,128)S(1)} %fetch.2), channel_id=1, replica_groups={{0,2,4,6,8,10,12,14},{16,18,20,22,24,26,28,30},{1,3,5,7,9,11,13,15},{17..., dimensions={0} | all-to-all | bytes 1048576 | tf_op jit(solution)/shard_map/cond/branch_1_fun/all_to_all | solution.py:251
  25.7 0.6 %first.1 = (f32[8,1,128]{2,1,0:T(1,128)S(1)}, f32[1,128]{1,0:T(1,128)S(1)}) custom-call(f32[8,1,128,128]{3,2,1,0:T(8,128)S(1)} %all_to_all.28.refs_0_, f32[8,128]{1,0:T(8,128)S(1)} %get-tuple-element.60.refs_1_), custom_call_target="tpu_custom_call" | custom-call | tf_op jit(solution)/shard_map/cond/branch_1_fun/first/pallas_call | solution.py:217
  26.3 1.3 %collective-permute-start = (f32[1,128]{1,0:T(1,128)S(1)}, f32[1,128]{1,0:T(1,128)S(1)}, u32[]{:S(2)}, u32[]{:S(2)}) collective-permute-start(f32[1,128]{1,0:T(1,128)S(1)} %get-tuple-element.55), channel_id=1, source_target_pairs={{0,16},{2,18},{4,20},{6,22},{8,24},{10,26},{12,28},{14,30},{1,17},... | collective-permute-start | bytes 1544 | tf_op jit(solution)/shard_map/ppermute | solution.py:293
  27.6 8.4 %conditional.3 = (f32[32,128]{1,0:T(8,128)S(1)}, f32[8,2,128,128]{3,2,1,0:T(8,128)S(1)}) conditional(s32[]{:T(128)} %convert_element_type.4, (s32[16,1,8]{2,1,0:T(1,128)S(1)}, s32[1,8]{1,0:T(1,128)S(1)}, s32[1,8]{1,0:T(1,128)S(1)}, bf16[64,128,128]{2,1,0:T(8,128)(2,1)S(1)}) %tuple.38, (f32[8,1,128]{2,1,0:T(1,128)S(1)}, s32[16,1,8]{2,1,0:T(1,128)S(1)}, ...), branch_computations={%region_2.3_spmd, %region_3.4_spmd} | conditional | bytes 2113556 | solution.py:294
  27.6 7.9 %all_to_all.30.refs_0_ = f32[8,1,128]{2,1,0:T(1,128)S(1)} all-to-all(f32[8,1,128]{2,1,0:T(1,128)S(1)} %get-tuple-element.37), channel_id=1, replica_groups={{0,2,4,6,8,10,12,14},{16,18,20,22,24,26,28,30},{1,3,5,7,9,11,13,15},{17..., dimensions={0} | all-to-all | bytes 8192 | tf_op jit(solution)/shard_map/cond/branch_1_fun/all_to_all | solution.py:251
  35.5 0.4 site_weights.1
  35.9 0.1 broadcast.13
  36.0 0.0 collective-permute-done.refs_2_
  36.1 8.8 %all_to_all.31 = f32[32,1,128]{2,1,0:T(1,128)S(1)} all-to-all(f32[32,1,128]{2,1,0:T(1,128)S(1)} %bitcast.10), channel_id=1, replica_groups=mesh['site'=16,'batch'=2] {'batch','site'}, dimensions={0} | all-to-all | bytes 32768 | tf_op jit(solution)/shard_map/all_to_all | solution.py:317
  44.9 0.6 %collect.1 = (f32[1,8]{1,0:T(1,128)}, f32[1,8]{1,0:T(1,128)}, f32[1,1]{1,0:T(1,128)}) custom-call(f32[32,128]{1,0:T(8,128)S(1)} %bitcast.11), custom_call_target="tpu_custom_call" | custom-call | tf_op jit(solution)/shard_map/collect/pallas_call | solution.py:217
  (1 shorter events, 0.0 us)
Async XLA Ops:
  1.9 12.9 %all-to-all-start.3 = ((s32[16,1,8]{2,1,0:T(1,128)}), s32[16,1,8]{2,1,0:T(1,128)S(1)}, u32[]{:S(2)}, u32[]{:S(2)}) async-start(s32[16,1,8]{2,1,0:T(1,128)} %broadcast_in_dim.12), calls=%async_computation.3 | async-start | bytes 16384 | tf_op jit(solution)/shard_map/all_to_all | solution.py:244
  10.7 1.6 %copy-start = (bf16[1,2,32,128,128]{4,3,2,1,0:T(8,128)(2,1)S(1)}, bf16[1,2,32,128,128]{4,3,2,1,0:T(8,128)(2,1)}, u32[]{:S(2)}) copy-start(bf16[1,2,32,128,128]{4,3,2,1,0:T(8,128)(2,1)} %param.8) | copy-start | bytes 6291460
  12.3 2.5 %copy-start.1 = (s32[1,8]{1,0:T(1,128)S(1)}, s32[1,8]{1,0:T(1,128)}, u32[]{:S(2)}) copy-start(s32[1,8]{1,0:T(1,128)} %param.11) | copy-start | bytes 100
  12.3 2.5 %copy-start.2 = (s32[8]{0:T(128)S(1)}, s32[8]{0:T(128)}, u32[]{:S(2)}) copy-start(s32[8]{0:T(128)} %param.10) | copy-start | bytes 100
  12.3 2.5 %copy-start.3 = (f32[8,128]{1,0:T(8,128)S(1)}, f32[8,128]{1,0:T(8,128)}, u32[]{:S(2)}) copy-start(f32[8,128]{1,0:T(8,128)} %param.9) | copy-start | bytes 12292
  26.3 9.7 %collective-permute-start = (f32[1,128]{1,0:T(1,128)S(1)}, f32[1,128]{1,0:T(1,128)S(1)}, u32[]{:S(2)}, u32[]{:S(2)}) collective-permute-start(f32[1,128]{1,0:T(1,128)S(1)} %get-tuple-element.55), channel_id=1, source_target_pairs={{0,16},{2,18},{4,20},{6,22},{8,24},{10,26},{12,28},{14,30},{1,17},... | collective-permute-start | bytes 1544 | tf_op jit(solution)/shard_map/ppermute | solution.py:293

commit v5 on v4

--- a/solution.py
+++ b/solution.py
@@ -8,7 +8,6 @@
 epsilon = 1e-06
 LANES = 128
 VMEM_BYTES = 24 << 20
-LEAD = 9
 
 
 def whole():
@@ -23,11 +22,10 @@
     return lax.broadcasted_iota(jnp.int32, shape, 0)
 
 
-def first_order(sites):
-    lead = sites * LEAD // 16
-    order = list(range(sites))
+def led_by(lead, count):
+    order = list(range(count))
     order[0], order[lead] = lead, 0
-    return order, lead
+    return order
 
 
 def swapped(index, lead):
@@ -70,23 +68,14 @@
             out[s, n] = table[picks[n][0, s]].astype(jnp.float32)
 
 
-def halves(x):
-    high = x.astype(jnp.bfloat16)
-    return high, (x - high.astype(jnp.float32)).astype(jnp.bfloat16)
-
-
 def times_exact(left, right):
     rows = left.shape[0]
+    high = left.astype(jnp.bfloat16)
+    low = (left - high.astype(jnp.float32)).astype(jnp.bfloat16)
     both = jnp.dot(
-        jnp.concatenate(halves(left), axis=0), right, preferred_element_type=jnp.float32
+        jnp.concatenate([high, low], axis=0), right, preferred_element_type=jnp.float32
     )
     return both[:rows] + both[rows:]
-
-
-def times(left, right):
-    high, low = halves(right)
-    part = jnp.dot(left.astype(jnp.bfloat16), low, preferred_element_type=jnp.float32)
-    return times_exact(left, high) + part
 
 
 def as_column(row):
@@ -100,31 +89,28 @@
 
 def vectors(blocks, vector, group):
     entering = [vector]
-    chosen = [blocks[k, 0].astype(jnp.bfloat16) for k in range(group)]
-    for k in range(0, group - 3, 4):
-        one, two = (
-            jnp.dot(chosen[j], chosen[j + 1], preferred_element_type=jnp.float32)
-            for j in (k, k + 2)
-        )
+    pairs = [
+        jnp.dot(
+            blocks[k, 0].astype(jnp.bfloat16),
+            blocks[k + 1, 0].astype(jnp.bfloat16),
+            preferred_element_type=jnp.float32,
+        )
+        for k in range(0, group - 1, 2)
+    ]
+    for k, pair in zip(range(0, group, 2), pairs):
         vector = entering[-1]
-        middle = row_times(vector, one)
-        entering += [
-            row_times(vector, blocks[k, 0]),
-            middle,
-            row_times(middle, blocks[k + 2, 0]),
-            row_times(vector, times(one, two)),
-        ]
-    while len(entering) <= group:
-        entering.append(row_times(entering[-1], blocks[len(entering) - 1, 0]))
+        entering += [row_times(vector, blocks[k, 0]), row_times(vector, pair)]
+    if group % 2:
+        entering.append(row_times(entering[-1], blocks[group - 1, 0]))
     return entering
 
 
-def first_kernel(group, blocks, start, entering, leaving):
+def first_kernel(group, back, blocks, start, entering, leaving):
     vector = start[pl.ds(lax.axis_index("site") % group, 1), :]
     found = vectors(blocks, vector, group)
     leaving[...] = found[-1]
     for k in range(group):
-        entering[k] = found[k]
+        entering[back.index(k)] = found[k]
 
 
 def products_kernel(group, blocks, product):
@@ -144,13 +130,13 @@
     return jnp.sum(row * row, axis=1, keepdims=True)
 
 
-def site_kernel(sectors, sites, lead, returned, heard, occupied, start_label, table, out):
+def site_kernel(sectors, sites, lead, back, returned, heard, occupied, start_label, table, out):
     place, batch = lax.axis_index("site"), lax.axis_index("batch")
     picks = picks_of(sectors, lead, heard, occupied, start_label)
     samples = returned.shape[0]
     found = [[], []]
     for s in range(samples):
-        column = as_column(returned[s])
+        column = as_column(returned[back.index(s)])
         for n in range(2):
             block = table[picks[n][0, s]].astype(jnp.float32)
             found[n].append(jnp.sum(column * block, axis=0, keepdims=True))
@@ -239,16 +225,18 @@
 
     table = keep(site_tensors.reshape(2 * sectors, width, width))
 
-    order, lead = first_order(sites)
+    lead = sites * 3 // 4
+    order = led_by(lead, sites)
     told = jnp.broadcast_to(occupations[:, None, :], (sites, 1, samples))
     heard = lax.all_to_all(told, "site", 0, 0, tiled=True, axis_index_groups=[order])
 
-    teams = [[g * group + k for k in range(group)] for g in range(groups)]
+    ahead, back = list(range(group)), led_by(min(2, group - 1), group)
     given = (heard, occupations, start_label[None, :], table)
     message_like = jax.ShapeDtypeStruct((everyone, LANES), f32)
 
-    def trade(blocks):
-        return lax.all_to_all(blocks, "site", 0, 0, tiled=True, axis_index_groups=teams)
+    def trade(parts, order):
+        teams = [[g * group + k for k in order] for g in range(groups)]
+        return lax.all_to_all(parts, "site", 0, 0, tiled=True, axis_index_groups=teams)
 
     def fetch(count):
         return call(
@@ -260,12 +248,12 @@
 
     def first():
         return call(
-            lambda *refs: first_kernel(group, *refs),
+            lambda *refs: first_kernel(group, back, *refs),
             (
                 jax.ShapeDtypeStruct((group, 1, width), f32),
                 jax.ShapeDtypeStruct((1, width), f32),
             ),
-            trade(fetch(1)),
+            trade(fetch(1), ahead),
             start_vector,
             name="first",
         )
@@ -275,16 +263,16 @@
 
     def second(entering):
         message = call(
-            lambda *refs: site_kernel(sectors, sites, lead, *refs),
+            lambda *refs: site_kernel(sectors, sites, lead, back, *refs),
             message_like,
-            trade(entering),
+            trade(entering, back),
             *given,
             name="site_weights",
         )
         return message, jnp.zeros((group, 2, width, width), f32)
 
     def later(entering):
-        return jnp.zeros(message_like.shape, f32), trade(fetch(2))
+        return jnp.zeros(message_like.shape, f32), trade(fetch(2), ahead)
 
     entering, leaving = lax.cond(here == 0, first, first_idle)
     vector = leaving

time: 45.8 us -> 45.3 us (0.989)
  no operation moved by 1% of the time
where the time goes in v5:
time: 45.3 us; the launch traced here: 45 us
  blocking collectives  27 us (60%)
  starting transfers between devices  10.1 us (22%)
  local copies, waits for them, and re-layouts  2.95 us (7%)
  waiting for transfers between devices  2.4 us (5%)
  Pallas kernels  1.81 us (4%)
  between operations  0.69 us (2%)
    all_to_all x2, blocking collectives, trade(): lax.all_to_all(parts, 'site', 0, 0, tiled=True, axis_index_groups=teams)  18.2 us
    all_to_all x1, blocking collectives, on_device(): reply = lax.all_to_all(message, ('batch', 'site'), 0, 0, tiled=True)  8.82 us
    all_to_all x1, starting transfers between devices, on_device(): lax.all_to_all(told, 'site', 0, 0, tiled=True, axis_index_groups=[order])  8.79 us
    all_to_all x1, waiting for transfers between devices, on_device(): lax.all_to_all(told, 'site', 0, 0, tiled=True, axis_index_groups=[order])  2.39 us
    pallas_call x5, Pallas kernels, call(): pl.pallas_call(kernel, in_specs=[whole()] * len(arrays), out_specs=out_sp...  1.66 us
    unnamed x8, local copies, waits for them, and re-layouts  1.6 us
    ppermute x1, starting transfers between devices, on_device(): vector = lax.ppermute(leaving, 'site', onward)  1.29 us
    broadcast_in_dim x1, local copies, waits for them, and re-layouts, on_device(): told = jnp.broadcast_to(occupations[:, None, :], (sites, 1, samples))  1.26 us
  transfers between devices with their start and end apart: 2, of which 1 were waited for; matrix products, arithmetic and copies ran while one was open for 0% of the time, Pallas kernels for 1%

profile of v5, /device:TPU:0, one launch (start us, length us, event | category | flops | bytes accessed | tf_op | source)
XLA Modules:
  0.0 45.0 jit_solution(6698083479525958181)
XLA Ops:
  0.6 1.3 %broadcast_in_dim.12 = s32[16,1,8]{2,1,0:T(1,128)} broadcast(s32[8]{0:T(128)} %bitcast.12), dimensions={2} | broadcast | bytes 544 | tf_op jit(solution)/shard_map/broadcast_in_dim | solution.py:230
  1.9 8.8 %all-to-all-start.3 = ((s32[16,1,8]{2,1,0:T(1,128)}), s32[16,1,8]{2,1,0:T(1,128)S(1)}, u32[]{:S(2)}, u32[]{:S(2)}) async-start(s32[16,1,8]{2,1,0:T(1,128)} %broadcast_in_dim.12), calls=%async_computation.3 | async-start | bytes 16384 | tf_op jit(solution)/shard_map/all_to_all | solution.py:231
  10.7 0.0 copy-start
  10.7 1.6 %copy-done = bf16[1,2,32,128,128]{4,3,2,1,0:T(8,128)(2,1)S(1)} copy-done((bf16[1,2,32,128,128]{4,3,2,1,0:T(8,128)(2,1)S(1)}, bf16[1,2,32,128,128]{4,3,2,1,0:T(8,128)(2,1)}, u32[]{:S(2)}) %copy-start) | copy-done | bytes 2097176
  12.3 0.0 copy-start.1
  12.3 0.0 copy-start.2
  12.3 0.0 copy-start.3
  12.3 0.1 keep.1
  12.4 2.4 %all-to-all-done.3.refs_3_ = s32[16,1,8]{2,1,0:T(1,128)S(1)} async-done(((s32[16,1,8]{2,1,0:T(1,128)}), s32[16,1,8]{2,1,0:T(1,128)S(1)}, u32[]{:S(2)}, u32[]{:S(2)}) %all-to-all-start.3) | async-done | bytes 544 | tf_op jit(solution)/shard_map/all_to_all | solution.py:231
  14.8 0.0 copy-done.1
  14.8 0.0 copy-done.2
  14.8 0.0 copy-done.3
  14.8 11.4 %conditional.2 = ((f32[8,1,128]{2,1,0:T(1,128)S(1)}, f32[1,128]{1,0:T(1,128)S(1)})) conditional(s32[]{:T(128)} %convert_element_type.4, () %tuple.24, (s32[16,1,8]{2,1,0:T(1,128)S(1)}, s32[1,8]{1,0:T(1,128)S(1)}, s32[1,8]{1,0:T(1,128)S(1)}, bf16[64,128,128]{2,1,0:T(8,128)(2,1)S(1)}, f32[8,128]{1,0:T(8,128)S(1)}) %tuple.40), branch_computations={%region_0.1_spmd, %region_1.2_spmd} | conditional | bytes 1048584 | solution.py:277
  14.9 0.2 fetch.2
  15.0 10.7 %all_to_all.28.refs_0_ = f32[8,1,128,128]{3,2,1,0:T(8,128)S(1)} all-to-all(f32[8,1,128,128]{3,2,1,0:T(8,128)S(1)} %fetch.2), channel_id=1, replica_groups={{0,2,4,6,8,10,12,14},{16,18,20,22,24,26,28,30},{1,3,5,7,9,11,13,15},{17..., dimensions={0} | all-to-all | bytes 1048576 | tf_op jit(solution)/shard_map/cond/branch_1_fun/all_to_all | solution.py:239
  25.7 0.5 %first.1 = (f32[8,1,128]{2,1,0:T(1,128)S(1)}, f32[1,128]{1,0:T(1,128)S(1)}) custom-call(f32[8,1,128,128]{3,2,1,0:T(8,128)S(1)} %all_to_all.28.refs_0_, f32[8,128]{1,0:T(8,128)S(1)} %get-tuple-element.60.refs_1_), custom_call_target="tpu_custom_call" | custom-call | tf_op jit(solution)/shard_map/cond/branch_1_fun/first/pallas_call | solution.py:203
  26.2 1.3 %collective-permute-start = (f32[1,128]{1,0:T(1,128)S(1)}, f32[1,128]{1,0:T(1,128)S(1)}, u32[]{:S(2)}, u32[]{:S(2)}) collective-permute-start(f32[1,128]{1,0:T(1,128)S(1)} %get-tuple-element.55), channel_id=1, source_target_pairs={{0,16},{2,18},{4,20},{6,22},{8,24},{10,26},{12,28},{14,30},{1,17},... | collective-permute-start | bytes 1544 | tf_op jit(solution)/shard_map/ppermute | solution.py:281
  27.5 8.0 %conditional.3 = (f32[32,128]{1,0:T(8,128)S(1)}, f32[8,2,128,128]{3,2,1,0:T(8,128)S(1)}) conditional(s32[]{:T(128)} %convert_element_type.4, (s32[16,1,8]{2,1,0:T(1,128)S(1)}, s32[1,8]{1,0:T(1,128)S(1)}, s32[1,8]{1,0:T(1,128)S(1)}, bf16[64,128,128]{2,1,0:T(8,128)(2,1)S(1)}) %tuple.38, (f32[8,1,128]{2,1,0:T(1,128)S(1)}, s32[16,1,8]{2,1,0:T(1,128)S(1)}, ...), branch_computations={%region_2.3_spmd, %region_3.4_spmd} | conditional | bytes 2113556 | solution.py:282
  27.5 7.5 %all_to_all.30.refs_0_ = f32[8,1,128]{2,1,0:T(1,128)S(1)} all-to-all(f32[8,1,128]{2,1,0:T(1,128)S(1)} %get-tuple-element.37), channel_id=1, replica_groups={{4,2,0,6,8,10,12,14},{20,18,16,22,24,26,28,30},{5,3,1,7,9,11,13,15},{21..., dimensions={0} | all-to-all | bytes 8192 | tf_op jit(solution)/shard_map/cond/branch_1_fun/all_to_all | solution.py:239
  35.0 0.4 site_weights.1
  35.4 0.1 broadcast.13
  35.5 0.0 collective-permute-done.refs_2_
  35.6 8.8 %all_to_all.31 = f32[32,1,128]{2,1,0:T(1,128)S(1)} all-to-all(f32[32,1,128]{2,1,0:T(1,128)S(1)} %bitcast.10), channel_id=1, replica_groups=mesh['site'=16,'batch'=2] {'batch','site'}, dimensions={0} | all-to-all | bytes 32768 | tf_op jit(solution)/shard_map/all_to_all | solution.py:305
  44.4 0.6 %collect.1 = (f32[1,8]{1,0:T(1,128)}, f32[1,8]{1,0:T(1,128)}, f32[1,1]{1,0:T(1,128)}) custom-call(f32[32,128]{1,0:T(8,128)S(1)} %bitcast.11), custom_call_target="tpu_custom_call" | custom-call | tf_op jit(solution)/shard_map/collect/pallas_call | solution.py:203
  (1 shorter events, 0.0 us)
Async XLA Ops:
  1.9 12.9 %all-to-all-start.3 = ((s32[16,1,8]{2,1,0:T(1,128)}), s32[16,1,8]{2,1,0:T(1,128)S(1)}, u32[]{:S(2)}, u32[]{:S(2)}) async-start(s32[16,1,8]{2,1,0:T(1,128)} %broadcast_in_dim.12), calls=%async_computation.3 | async-start | bytes 16384 | tf_op jit(solution)/shard_map/all_to_all | solution.py:231
  10.7 1.6 %copy-start = (bf16[1,2,32,128,128]{4,3,2,1,0:T(8,128)(2,1)S(1)}, bf16[1,2,32,128,128]{4,3,2,1,0:T(8,128)(2,1)}, u32[]{:S(2)}) copy-start(bf16[1,2,32,128,128]{4,3,2,1,0:T(8,128)(2,1)} %param.8) | copy-start | bytes 6291460
  12.3 2.6 %copy-start.1 = (s32[1,8]{1,0:T(1,128)S(1)}, s32[1,8]{1,0:T(1,128)}, u32[]{:S(2)}) copy-start(s32[1,8]{1,0:T(1,128)} %param.11) | copy-start | bytes 100
  12.3 2.6 %copy-start.2 = (s32[8]{0:T(128)S(1)}, s32[8]{0:T(128)}, u32[]{:S(2)}) copy-start(s32[8]{0:T(128)} %param.10) | copy-start | bytes 100
  12.3 2.6 %copy-start.3 = (f32[8,128]{1,0:T(8,128)S(1)}, f32[8,128]{1,0:T(8,128)}, u32[]{:S(2)}) copy-start(f32[8,128]{1,0:T(8,128)} %param.9) | copy-start | bytes 12292
  26.2 9.3 %collective-permute-start = (f32[1,128]{1,0:T(1,128)S(1)}, f32[1,128]{1,0:T(1,128)S(1)}, u32[]{:S(2)}, u32[]{:S(2)}) collective-permute-start(f32[1,128]{1,0:T(1,128)S(1)} %get-tuple-element.55), channel_id=1, source_target_pairs={{0,16},{2,18},{4,20},{6,22},{8,24},{10,26},{12,28},{14,30},{1,17},... | collective-permute-start | bytes 1544 | tf_op jit(solution)/shard_map/ppermute | solution.py:281

commit v6 on v5

--- a/solution.py
+++ b/solution.py
@@ -88,20 +88,27 @@
 
 
 def vectors(blocks, vector, group):
+    chosen = [blocks[k, 0].astype(jnp.bfloat16) for k in range(group)]
     entering = [vector]
-    pairs = [
-        jnp.dot(
-            blocks[k, 0].astype(jnp.bfloat16),
-            blocks[k + 1, 0].astype(jnp.bfloat16),
-            preferred_element_type=jnp.float32,
-        )
-        for k in range(0, group - 1, 2)
-    ]
-    for k, pair in zip(range(0, group, 2), pairs):
-        vector = entering[-1]
-        entering += [row_times(vector, blocks[k, 0]), row_times(vector, pair)]
+    column = as_column(vector)
+    for k in range(0, group - 1, 2):
+        entering.append(jnp.sum(column * blocks[k, 0], axis=0, keepdims=True))
+        if k % 4 == 0:
+            pair = jnp.dot(chosen[k], chosen[k + 1], preferred_element_type=jnp.float32)
+            entering.append(jnp.sum(column * pair, axis=0, keepdims=True))
+            column = as_column(entering[-1])
+        else:
+            turned = lax.dot_general(
+                chosen[k + 1],
+                chosen[k],
+                (((0,), (1,)), ((), ())),
+                preferred_element_type=jnp.float32,
+            )
+            after = jnp.sum(turned * entering[-2], axis=1, keepdims=True)
+            column = jnp.broadcast_to(after, turned.shape)
+            entering.append(column.T[0:1, :])
     if group % 2:
-        entering.append(row_times(entering[-1], blocks[group - 1, 0]))
+        entering.append(jnp.sum(column * blocks[group - 1, 0], axis=0, keepdims=True))
     return entering
 
 

time: 45.3 us -> 45.3 us (level)
  no operation moved by 1% of the time
where the time goes in v6:
time: 45.3 us; the launch traced here: 45 us
  blocking collectives  27 us (60%)
  starting transfers between devices  10.1 us (22%)
  local copies, waits for them, and re-layouts  2.95 us (7%)
  waiting for transfers between devices  2.4 us (5%)
  Pallas kernels  1.82 us (4%)
  between operations  0.68 us (2%)
    all_to_all x2, blocking collectives, trade(): lax.all_to_all(parts, 'site', 0, 0, tiled=True, axis_index_groups=teams)  18.2 us
    all_to_all x1, blocking collectives, on_device(): reply = lax.all_to_all(message, ('batch', 'site'), 0, 0, tiled=True)  8.82 us
    all_to_all x1, starting transfers between devices, on_device(): lax.all_to_all(told, 'site', 0, 0, tiled=True, axis_index_groups=[order])  8.79 us
    all_to_all x1, waiting for transfers between devices, on_device(): lax.all_to_all(told, 'site', 0, 0, tiled=True, axis_index_groups=[order])  2.39 us
    pallas_call x5, Pallas kernels, call(): pl.pallas_call(kernel, in_specs=[whole()] * len(arrays), out_specs=out_sp...  1.67 us
    unnamed x8, local copies, waits for them, and re-layouts  1.6 us
    ppermute x1, starting transfers between devices, on_device(): vector = lax.ppermute(leaving, 'site', onward)  1.29 us
    broadcast_in_dim x1, local copies, waits for them, and re-layouts, on_device(): told = jnp.broadcast_to(occupations[:, None, :], (sites, 1, samples))  1.26 us
  transfers between devices with their start and end apart: 2, of which 1 were waited for; matrix products, arithmetic and copies ran while one was open for 0% of the time, Pallas kernels for 1%

profile of v6, /device:TPU:0, one launch (start us, length us, event | category | flops | bytes accessed | tf_op | source)
XLA Modules:
  0.0 45.0 jit_solution(8571745717428300516)
XLA Ops:
  0.6 1.3 %broadcast_in_dim.12 = s32[16,1,8]{2,1,0:T(1,128)} broadcast(s32[8]{0:T(128)} %bitcast.12), dimensions={2} | broadcast | bytes 544 | tf_op jit(solution)/shard_map/broadcast_in_dim | solution.py:237
  1.9 8.8 %all-to-all-start.3 = ((s32[16,1,8]{2,1,0:T(1,128)}), s32[16,1,8]{2,1,0:T(1,128)S(1)}, u32[]{:S(2)}, u32[]{:S(2)}) async-start(s32[16,1,8]{2,1,0:T(1,128)} %broadcast_in_dim.12), calls=%async_computation.3 | async-start | bytes 16384 | tf_op jit(solution)/shard_map/all_to_all | solution.py:238
  10.7 0.0 copy-start
  10.7 1.6 %copy-done = bf16[1,2,32,128,128]{4,3,2,1,0:T(8,128)(2,1)S(1)} copy-done((bf16[1,2,32,128,128]{4,3,2,1,0:T(8,128)(2,1)S(1)}, bf16[1,2,32,128,128]{4,3,2,1,0:T(8,128)(2,1)}, u32[]{:S(2)}) %copy-start) | copy-done | bytes 2097176
  12.3 0.0 copy-start.1
  12.3 0.0 copy-start.2
  12.3 0.0 copy-start.3
  12.3 0.1 keep.1
  12.4 2.4 %all-to-all-done.3.refs_3_ = s32[16,1,8]{2,1,0:T(1,128)S(1)} async-done(((s32[16,1,8]{2,1,0:T(1,128)}), s32[16,1,8]{2,1,0:T(1,128)S(1)}, u32[]{:S(2)}, u32[]{:S(2)}) %all-to-all-start.3) | async-done | bytes 544 | tf_op jit(solution)/shard_map/all_to_all | solution.py:238
  14.8 0.0 copy-done.1
  14.8 0.0 copy-done.2
  14.8 0.0 copy-done.3
  14.8 11.4 %conditional.2 = ((f32[8,1,128]{2,1,0:T(1,128)S(1)}, f32[1,128]{1,0:T(1,128)S(1)})) conditional(s32[]{:T(128)} %convert_element_type.4, () %tuple.24, (s32[16,1,8]{2,1,0:T(1,128)S(1)}, s32[1,8]{1,0:T(1,128)S(1)}, s32[1,8]{1,0:T(1,128)S(1)}, bf16[64,128,128]{2,1,0:T(8,128)(2,1)S(1)}, f32[8,128]{1,0:T(8,128)S(1)}) %tuple.40), branch_computations={%region_0.1_spmd, %region_1.2_spmd} | conditional | bytes 1048584 | solution.py:284
  14.9 0.2 fetch.2
  15.0 10.7 %all_to_all.28.refs_0_ = f32[8,1,128,128]{3,2,1,0:T(8,128)S(1)} all-to-all(f32[8,1,128,128]{3,2,1,0:T(8,128)S(1)} %fetch.2), channel_id=1, replica_groups={{0,2,4,6,8,10,12,14},{16,18,20,22,24,26,28,30},{1,3,5,7,9,11,13,15},{17..., dimensions={0} | all-to-all | bytes 1048576 | tf_op jit(solution)/shard_map/cond/branch_1_fun/all_to_all | solution.py:246
  25.7 0.5 %first.1 = (f32[8,1,128]{2,1,0:T(1,128)S(1)}, f32[1,128]{1,0:T(1,128)S(1)}) custom-call(f32[8,1,128,128]{3,2,1,0:T(8,128)S(1)} %all_to_all.28.refs_0_, f32[8,128]{1,0:T(8,128)S(1)} %get-tuple-element.60.refs_1_), custom_call_target="tpu_custom_call" | custom-call | tf_op jit(solution)/shard_map/cond/branch_1_fun/first/pallas_call | solution.py:210
  26.2 1.3 %collective-permute-start = (f32[1,128]{1,0:T(1,128)S(1)}, f32[1,128]{1,0:T(1,128)S(1)}, u32[]{:S(2)}, u32[]{:S(2)}) collective-permute-start(f32[1,128]{1,0:T(1,128)S(1)} %get-tuple-element.55), channel_id=1, source_target_pairs={{0,16},{2,18},{4,20},{6,22},{8,24},{10,26},{12,28},{14,30},{1,17},... | collective-permute-start | bytes 1544 | tf_op jit(solution)/shard_map/ppermute | solution.py:288
  27.5 8.0 %conditional.3 = (f32[32,128]{1,0:T(8,128)S(1)}, f32[8,2,128,128]{3,2,1,0:T(8,128)S(1)}) conditional(s32[]{:T(128)} %convert_element_type.4, (s32[16,1,8]{2,1,0:T(1,128)S(1)}, s32[1,8]{1,0:T(1,128)S(1)}, s32[1,8]{1,0:T(1,128)S(1)}, bf16[64,128,128]{2,1,0:T(8,128)(2,1)S(1)}) %tuple.38, (f32[8,1,128]{2,1,0:T(1,128)S(1)}, s32[16,1,8]{2,1,0:T(1,128)S(1)}, ...), branch_computations={%region_2.3_spmd, %region_3.4_spmd} | conditional | bytes 2113556 | solution.py:289
  27.5 7.5 %all_to_all.30.refs_0_ = f32[8,1,128]{2,1,0:T(1,128)S(1)} all-to-all(f32[8,1,128]{2,1,0:T(1,128)S(1)} %get-tuple-element.37), channel_id=1, replica_groups={{4,2,0,6,8,10,12,14},{20,18,16,22,24,26,28,30},{5,3,1,7,9,11,13,15},{21..., dimensions={0} | all-to-all | bytes 8192 | tf_op jit(solution)/shard_map/cond/branch_1_fun/all_to_all | solution.py:246
  35.0 0.4 site_weights.1
  35.4 0.1 broadcast.13
  35.5 0.0 collective-permute-done.refs_2_
  35.6 8.8 %all_to_all.31 = f32[32,1,128]{2,1,0:T(1,128)S(1)} all-to-all(f32[32,1,128]{2,1,0:T(1,128)S(1)} %bitcast.10), channel_id=1, replica_groups=mesh['site'=16,'batch'=2] {'batch','site'}, dimensions={0} | all-to-all | bytes 32768 | tf_op jit(solution)/shard_map/all_to_all | solution.py:312
  44.4 0.6 %collect.1 = (f32[1,8]{1,0:T(1,128)}, f32[1,8]{1,0:T(1,128)}, f32[1,1]{1,0:T(1,128)}) custom-call(f32[32,128]{1,0:T(8,128)S(1)} %bitcast.11), custom_call_target="tpu_custom_call" | custom-call | tf_op jit(solution)/shard_map/collect/pallas_call | solution.py:210
  (1 shorter events, 0.0 us)
Async XLA Ops:
  1.9 12.9 %all-to-all-start.3 = ((s32[16,1,8]{2,1,0:T(1,128)}), s32[16,1,8]{2,1,0:T(1,128)S(1)}, u32[]{:S(2)}, u32[]{:S(2)}) async-start(s32[16,1,8]{2,1,0:T(1,128)} %broadcast_in_dim.12), calls=%async_computation.3 | async-start | bytes 16384 | tf_op jit(solution)/shard_map/all_to_all | solution.py:238
  10.7 1.6 %copy-start = (bf16[1,2,32,128,128]{4,3,2,1,0:T(8,128)(2,1)S(1)}, bf16[1,2,32,128,128]{4,3,2,1,0:T(8,128)(2,1)}, u32[]{:S(2)}) copy-start(bf16[1,2,32,128,128]{4,3,2,1,0:T(8,128)(2,1)} %param.8) | copy-start | bytes 6291460
  12.3 2.6 %copy-start.1 = (s32[1,8]{1,0:T(1,128)S(1)}, s32[1,8]{1,0:T(1,128)}, u32[]{:S(2)}) copy-start(s32[1,8]{1,0:T(1,128)} %param.11) | copy-start | bytes 100
  12.3 2.6 %copy-start.2 = (s32[8]{0:T(128)S(1)}, s32[8]{0:T(128)}, u32[]{:S(2)}) copy-start(s32[8]{0:T(128)} %param.10) | copy-start | bytes 100
  12.3 2.6 %copy-start.3 = (f32[8,128]{1,0:T(8,128)S(1)}, f32[8,128]{1,0:T(8,128)}, u32[]{:S(2)}) copy-start(f32[8,128]{1,0:T(8,128)} %param.9) | copy-start | bytes 12292
  26.2 9.3 %collective-permute-start = (f32[1,128]{1,0:T(1,128)S(1)}, f32[1,128]{1,0:T(1,128)S(1)}, u32[]{:S(2)}, u32[]{:S(2)}) collective-permute-start(f32[1,128]{1,0:T(1,128)S(1)} %get-tuple-element.55), channel_id=1, source_target_pairs={{0,16},{2,18},{4,20},{6,22},{8,24},{10,26},{12,28},{14,30},{1,17},... | collective-permute-start | bytes 1544 | tf_op jit(solution)/shard_map/ppermute | solution.py:288

commit v7 on v6

--- a/solution.py
+++ b/solution.py
@@ -61,8 +61,9 @@
     return chosen, label + sectors - occupied[...] * sectors
 
 
-def fetch_kernel(sectors, lead, heard, occupied, start_label, table, out):
+def fetch_kernel(sectors, lead, heard, occupied, start_label, table, out, picked):
     picks = picks_of(sectors, lead, heard, occupied, start_label)
+    picked[0:1, :], picked[1:2, :] = picks
     for s in range(out.shape[0]):
         for n in range(out.shape[1]):
             out[s, n] = table[picks[n][0, s]].astype(jnp.float32)
@@ -137,9 +138,9 @@
     return jnp.sum(row * row, axis=1, keepdims=True)
 
 
-def site_kernel(sectors, sites, lead, back, returned, heard, occupied, start_label, table, out):
+def site_kernel(sites, back, returned, picked, occupied, table, out):
     place, batch = lax.axis_index("site"), lax.axis_index("batch")
-    picks = picks_of(sectors, lead, heard, occupied, start_label)
+    picks = [picked[n : n + 1, :] for n in range(2)]
     samples = returned.shape[0]
     found = [[], []]
     for s in range(samples):
@@ -248,45 +249,56 @@
     def fetch(count):
         return call(
             lambda *refs: fetch_kernel(sectors, lead, *refs),
-            jax.ShapeDtypeStruct((samples, count, width, width), f32),
+            (
+                jax.ShapeDtypeStruct((samples, count, width, width), f32),
+                jax.ShapeDtypeStruct((2, samples), jnp.int32),
+            ),
             *given,
             name="fetch",
         )
 
     def first():
-        return call(
+        blocks, picked = fetch(1)
+        entering, leaving = call(
             lambda *refs: first_kernel(group, back, *refs),
             (
                 jax.ShapeDtypeStruct((group, 1, width), f32),
                 jax.ShapeDtypeStruct((1, width), f32),
             ),
-            trade(fetch(1), ahead),
+            trade(blocks, ahead),
             start_vector,
             name="first",
         )
+        return entering, leaving, picked
 
     def first_idle():
-        return jnp.zeros((group, 1, width), f32), jnp.zeros((1, width), f32)
-
-    def second(entering):
+        return (
+            jnp.zeros((group, 1, width), f32),
+            jnp.zeros((1, width), f32),
+            jnp.zeros((2, samples), jnp.int32),
+        )
+
+    def second(entering, picked):
         message = call(
-            lambda *refs: site_kernel(sectors, sites, lead, back, *refs),
+            lambda *refs: site_kernel(sites, back, *refs),
             message_like,
             trade(entering, back),
-            *given,
+            picked,
+            occupations,
+            table,
             name="site_weights",
         )
         return message, jnp.zeros((group, 2, width, width), f32)
 
-    def later(entering):
-        return jnp.zeros(message_like.shape, f32), trade(fetch(2), ahead)
-
-    entering, leaving = lax.cond(here == 0, first, first_idle)
+    def later(entering, picked):
+        return jnp.zeros(message_like.shape, f32), trade(fetch(2)[0], ahead)
+
+    entering, leaving, picked = lax.cond(here == 0, first, first_idle)
     vector = leaving
     if groups > 1:
         onward = [(i, i + group) for i in range(group)]
         vector = lax.ppermute(leaving, "site", onward)
-    from_site, blocks = lax.cond(here == 0, second, later, entering)
+    from_site, blocks = lax.cond(here == 0, second, later, entering, picked)
     if groups > 2:
         product = call(
             lambda *refs: products_kernel(group, *refs),

time: 45.3 us -> 45.3 us (level)
  no operation moved by 1% of the time
where the time goes in v7:
time: 45.3 us; the launch traced here: 45 us
  blocking collectives  27 us (60%)
  starting transfers between devices  10.1 us (22%)
  local copies, waits for them, and re-layouts  2.94 us (6%)
  waiting for transfers between devices  2.39 us (5%)
  Pallas kernels  1.79 us (4%)
  between operations  0.68 us (2%)
    all_to_all x2, blocking collectives, trade(): lax.all_to_all(parts, 'site', 0, 0, tiled=True, axis_index_groups=teams)  18.2 us
    all_to_all x1, blocking collectives, on_device(): reply = lax.all_to_all(message, ('batch', 'site'), 0, 0, tiled=True)  8.82 us
    all_to_all x1, starting transfers between devices, on_device(): lax.all_to_all(told, 'site', 0, 0, tiled=True, axis_index_groups=[order])  8.79 us
    all_to_all x1, waiting for transfers between devices, on_device(): lax.all_to_all(told, 'site', 0, 0, tiled=True, axis_index_groups=[order])  2.39 us
    pallas_call x5, Pallas kernels, call(): pl.pallas_call(kernel, in_specs=[whole()] * len(arrays), out_specs=out_sp...  1.64 us
    unnamed x8, local copies, waits for them, and re-layouts  1.6 us
    ppermute x1, starting transfers between devices, on_device(): vector = lax.ppermute(leaving, 'site', onward)  1.29 us
    broadcast_in_dim x1, local copies, waits for them, and re-layouts, on_device(): told = jnp.broadcast_to(occupations[:, None, :], (sites, 1, samples))  1.25 us
  transfers between devices with their start and end apart: 2, of which 1 were waited for; matrix products, arithmetic and copies ran while one was open for 0% of the time, Pallas kernels for 1%

profile of v7, /device:TPU:0, one launch (start us, length us, event | category | flops | bytes accessed | tf_op | source)
XLA Modules:
  0.0 45.0 jit_solution(16068761743230887722)
XLA Ops:
  0.6 1.3 %broadcast_in_dim.12 = s32[16,1,8]{2,1,0:T(1,128)} broadcast(s32[8]{0:T(128)} %bitcast.12), dimensions={2} | broadcast | bytes 544 | tf_op jit(solution)/shard_map/broadcast_in_dim | solution.py:238
  1.9 8.8 %all-to-all-start.3 = ((s32[16,1,8]{2,1,0:T(1,128)}), s32[16,1,8]{2,1,0:T(1,128)S(1)}, u32[]{:S(2)}, u32[]{:S(2)}) async-start(s32[16,1,8]{2,1,0:T(1,128)} %broadcast_in_dim.12), calls=%async_computation.3 | async-start | bytes 16384 | tf_op jit(solution)/shard_map/all_to_all | solution.py:239
  10.7 0.0 copy-start
  10.7 1.6 %copy-done = bf16[1,2,32,128,128]{4,3,2,1,0:T(8,128)(2,1)S(1)} copy-done((bf16[1,2,32,128,128]{4,3,2,1,0:T(8,128)(2,1)S(1)}, bf16[1,2,32,128,128]{4,3,2,1,0:T(8,128)(2,1)}, u32[]{:S(2)}) %copy-start) | copy-done | bytes 2097176
  12.3 0.0 copy-start.1
  12.3 0.0 copy-start.2
  12.3 0.0 copy-start.3
  12.3 0.1 keep.1
  12.4 2.4 %all-to-all-done.3.refs_3_ = s32[16,1,8]{2,1,0:T(1,128)S(1)} async-done(((s32[16,1,8]{2,1,0:T(1,128)}), s32[16,1,8]{2,1,0:T(1,128)S(1)}, u32[]{:S(2)}, u32[]{:S(2)}) %all-to-all-start.3) | async-done | bytes 544 | tf_op jit(solution)/shard_map/all_to_all | solution.py:239
  14.8 0.0 copy-done.1
  14.8 0.0 copy-done.2
  14.8 0.0 copy-done.3
  14.8 11.4 %conditional.2 = (f32[8,1,128]{2,1,0:T(1,128)S(1)}, f32[1,128]{1,0:T(1,128)S(1)}, s32[2,8]{1,0:T(2,128)S(1)}) conditional(s32[]{:T(128)} %convert_element_type.4, () %tuple.25, (s32[16,1,8]{2,1,0:T(1,128)S(1)}, s32[1,8]{1,0:T(1,128)S(1)}, s32[1,8]{1,0:T(1,128)S(1)}, bf16[64,128,128]{2,1,0:T(8,128)(2,1)S(1)}, f32[8,128]{1,0:T(8,128)S(1)}) %tuple.37), branch_computations={%region_0.1_spmd, %region_1.2_spmd} | conditional | bytes 1048600 | solution.py:296
  14.8 0.2 fetch.2
  15.0 10.7 %all_to_all.28.refs_0_ = f32[8,1,128,128]{3,2,1,0:T(8,128)S(1)} all-to-all(f32[8,1,128,128]{3,2,1,0:T(8,128)S(1)} %get-tuple-element.30), channel_id=1, replica_groups={{0,2,4,6,8,10,12,14},{16,18,20,22,24,26,28,30},{1,3,5,7,9,11,13,15},{17..., dimensions={0} | all-to-all | bytes 1048576 | tf_op jit(solution)/shard_map/cond/branch_1_fun/all_to_all | solution.py:247
  25.7 0.5 %first.1 = (f32[8,1,128]{2,1,0:T(1,128)S(1)}, f32[1,128]{1,0:T(1,128)S(1)}) custom-call(f32[8,1,128,128]{3,2,1,0:T(8,128)S(1)} %all_to_all.28.refs_0_, f32[8,128]{1,0:T(8,128)S(1)} %get-tuple-element.64.refs_1_), custom_call_target="tpu_custom_call" | custom-call | tf_op jit(solution)/shard_map/cond/branch_1_fun/first/pallas_call | solution.py:211
  26.2 1.3 %collective-permute-start = (f32[1,128]{1,0:T(1,128)S(1)}, f32[1,128]{1,0:T(1,128)S(1)}, u32[]{:S(2)}, u32[]{:S(2)}) collective-permute-start(f32[1,128]{1,0:T(1,128)S(1)} %get-tuple-element.59), channel_id=1, source_target_pairs={{0,16},{2,18},{4,20},{6,22},{8,24},{10,26},{12,28},{14,30},{1,17},... | collective-permute-start | bytes 1544 | tf_op jit(solution)/shard_map/ppermute | solution.py:300
  27.5 8.0 %conditional.3 = (f32[32,128]{1,0:T(8,128)S(1)}, f32[8,2,128,128]{3,2,1,0:T(8,128)S(1)}) conditional(s32[]{:T(128)} %convert_element_type.4, (s32[16,1,8]{2,1,0:T(1,128)S(1)}, s32[1,8]{1,0:T(1,128)S(1)}, s32[1,8]{1,0:T(1,128)S(1)}, bf16[64,128,128]{2,1,0:T(8,128)(2,1)S(1)}) %tuple.38, (f32[8,1,128]{2,1,0:T(1,128)S(1)}, s32[2,8]{1,0:T(2,128)S(1)}, ...), branch_computations={%region_2.3_spmd, %region_3.4_spmd} | conditional | bytes 2113556 | solution.py:301
  27.5 7.5 %all_to_all.30.refs_0_ = f32[8,1,128]{2,1,0:T(1,128)S(1)} all-to-all(f32[8,1,128]{2,1,0:T(1,128)S(1)} %get-tuple-element.40), channel_id=1, replica_groups={{4,2,0,6,8,10,12,14},{20,18,16,22,24,26,28,30},{5,3,1,7,9,11,13,15},{21..., dimensions={0} | all-to-all | bytes 8192 | tf_op jit(solution)/shard_map/cond/branch_1_fun/all_to_all | solution.py:247
  35.0 0.4 site_weights.1
  35.4 0.1 broadcast.16
  35.5 0.0 collective-permute-done.refs_2_
  35.6 8.8 %all_to_all.31 = f32[32,1,128]{2,1,0:T(1,128)S(1)} all-to-all(f32[32,1,128]{2,1,0:T(1,128)S(1)} %bitcast.10), channel_id=1, replica_groups=mesh['site'=16,'batch'=2] {'batch','site'}, dimensions={0} | all-to-all | bytes 32768 | tf_op jit(solution)/shard_map/all_to_all | solution.py:324
  44.4 0.6 %collect.1 = (f32[1,8]{1,0:T(1,128)}, f32[1,8]{1,0:T(1,128)}, f32[1,1]{1,0:T(1,128)}) custom-call(f32[32,128]{1,0:T(8,128)S(1)} %bitcast.11), custom_call_target="tpu_custom_call" | custom-call | tf_op jit(solution)/shard_map/collect/pallas_call | solution.py:211
  (1 shorter events, 0.0 us)
Async XLA Ops:
  1.9 12.9 %all-to-all-start.3 = ((s32[16,1,8]{2,1,0:T(1,128)}), s32[16,1,8]{2,1,0:T(1,128)S(1)}, u32[]{:S(2)}, u32[]{:S(2)}) async-start(s32[16,1,8]{2,1,0:T(1,128)} %broadcast_in_dim.12), calls=%async_computation.3 | async-start | bytes 16384 | tf_op jit(solution)/shard_map/all_to_all | solution.py:239
  10.7 1.6 %copy-start = (bf16[1,2,32,128,128]{4,3,2,1,0:T(8,128)(2,1)S(1)}, bf16[1,2,32,128,128]{4,3,2,1,0:T(8,128)(2,1)}, u32[]{:S(2)}) copy-start(bf16[1,2,32,128,128]{4,3,2,1,0:T(8,128)(2,1)} %param.8) | copy-start | bytes 6291460
  12.3 2.6 %copy-start.1 = (s32[1,8]{1,0:T(1,128)S(1)}, s32[1,8]{1,0:T(1,128)}, u32[]{:S(2)}) copy-start(s32[1,8]{1,0:T(1,128)} %param.11) | copy-start | bytes 100
  12.3 2.6 %copy-start.2 = (f32[8,128]{1,0:T(8,128)S(1)}, f32[8,128]{1,0:T(8,128)}, u32[]{:S(2)}) copy-start(f32[8,128]{1,0:T(8,128)} %param.9) | copy-start | bytes 12292
  12.3 2.6 %copy-start.3 = (s32[8]{0:T(128)S(1)}, s32[8]{0:T(128)}, u32[]{:S(2)}) copy-start(s32[8]{0:T(128)} %param.10) | copy-start | bytes 100
  26.2 9.3 %collective-permute-start = (f32[1,128]{1,0:T(1,128)S(1)}, f32[1,128]{1,0:T(1,128)S(1)}, u32[]{:S(2)}, u32[]{:S(2)}) collective-permute-start(f32[1,128]{1,0:T(1,128)S(1)} %get-tuple-element.59), channel_id=1, source_target_pairs={{0,16},{2,18},{4,20},{6,22},{8,24},{10,26},{12,28},{14,30},{1,17},... | collective-permute-start | bytes 1544 | tf_op jit(solution)/shard_map/ppermute | solution.py:300

commit v8 on v7

--- a/solution.py
+++ b/solution.py
@@ -233,7 +233,7 @@
 
     table = keep(site_tensors.reshape(2 * sectors, width, width))
 
-    lead = sites * 3 // 4
+    lead = sites * 9 // 16
     order = led_by(lead, sites)
     told = jnp.broadcast_to(occupations[:, None, :], (sites, 1, samples))
     heard = lax.all_to_all(told, "site", 0, 0, tiled=True, axis_index_groups=[order])

time: 45.3 us -> 45.3 us (level)
  no operation moved by 1% of the time
where the time goes in v8:
time: 45.3 us; the launch traced here: 45 us
  blocking collectives  27 us (60%)
  starting transfers between devices  10.1 us (22%)
  local copies, waits for them, and re-layouts  2.94 us (6%)
  waiting for transfers between devices  2.38 us (5%)
  Pallas kernels  1.79 us (4%)
  between operations  0.68 us (2%)
    all_to_all x2, blocking collectives, trade(): lax.all_to_all(parts, 'site', 0, 0, tiled=True, axis_index_groups=teams)  18.2 us
    all_to_all x1, blocking collectives, on_device(): reply = lax.all_to_all(message, ('batch', 'site'), 0, 0, tiled=True)  8.82 us
    all_to_all x1, starting transfers between devices, on_device(): lax.all_to_all(told, 'site', 0, 0, tiled=True, axis_index_groups=[order])  8.79 us
    all_to_all x1, waiting for transfers between devices, on_device(): lax.all_to_all(told, 'site', 0, 0, tiled=True, axis_index_groups=[order])  2.37 us
    pallas_call x5, Pallas kernels, call(): pl.pallas_call(kernel, in_specs=[whole()] * len(arrays), out_specs=out_sp...  1.64 us
    unnamed x8, local copies, waits for them, and re-layouts  1.6 us
    ppermute x1, starting transfers between devices, on_device(): vector = lax.ppermute(leaving, 'site', onward)  1.29 us
    broadcast_in_dim x1, local copies, waits for them, and re-layouts, on_device(): told = jnp.broadcast_to(occupations[:, None, :], (sites, 1, samples))  1.25 us
  transfers between devices with their start and end apart: 2, of which 1 were waited for; matrix products, arithmetic and copies ran while one was open for 0% of the time, Pallas kernels for 1%

profile of v8, /device:TPU:0, one launch (start us, length us, event | category | flops | bytes accessed | tf_op | source)
XLA Modules:
  0.0 45.0 jit_solution(6211259943342163372)
XLA Ops:
  0.6 1.3 %broadcast_in_dim.12 = s32[16,1,8]{2,1,0:T(1,128)} broadcast(s32[8]{0:T(128)} %bitcast.12), dimensions={2} | broadcast | bytes 544 | tf_op jit(solution)/shard_map/broadcast_in_dim | solution.py:238
  1.9 8.8 %all-to-all-start.3 = ((s32[16,1,8]{2,1,0:T(1,128)}), s32[16,1,8]{2,1,0:T(1,128)S(1)}, u32[]{:S(2)}, u32[]{:S(2)}) async-start(s32[16,1,8]{2,1,0:T(1,128)} %broadcast_in_dim.12), calls=%async_computation.3 | async-start | bytes 16384 | tf_op jit(solution)/shard_map/all_to_all | solution.py:239
  10.7 0.0 copy-start
  10.7 1.6 %copy-done = bf16[1,2,32,128,128]{4,3,2,1,0:T(8,128)(2,1)S(1)} copy-done((bf16[1,2,32,128,128]{4,3,2,1,0:T(8,128)(2,1)S(1)}, bf16[1,2,32,128,128]{4,3,2,1,0:T(8,128)(2,1)}, u32[]{:S(2)}) %copy-start) | copy-done | bytes 2097176
  12.3 0.0 copy-start.1
  12.3 0.0 copy-start.2
  12.3 0.0 copy-start.3
  12.3 0.1 keep.1
  12.4 2.4 %all-to-all-done.3.refs_3_ = s32[16,1,8]{2,1,0:T(1,128)S(1)} async-done(((s32[16,1,8]{2,1,0:T(1,128)}), s32[16,1,8]{2,1,0:T(1,128)S(1)}, u32[]{:S(2)}, u32[]{:S(2)}) %all-to-all-start.3) | async-done | bytes 544 | tf_op jit(solution)/shard_map/all_to_all | solution.py:239
  14.8 0.0 copy-done.1
  14.8 0.0 copy-done.2
  14.8 0.0 copy-done.3
  14.8 11.4 %conditional.2 = (f32[8,1,128]{2,1,0:T(1,128)S(1)}, f32[1,128]{1,0:T(1,128)S(1)}, s32[2,8]{1,0:T(2,128)S(1)}) conditional(s32[]{:T(128)} %convert_element_type.4, () %tuple.25, (s32[16,1,8]{2,1,0:T(1,128)S(1)}, s32[1,8]{1,0:T(1,128)S(1)}, s32[1,8]{1,0:T(1,128)S(1)}, bf16[64,128,128]{2,1,0:T(8,128)(2,1)S(1)}, f32[8,128]{1,0:T(8,128)S(1)}) %tuple.37), branch_computations={%region_0.1_spmd, %region_1.2_spmd} | conditional | bytes 1048600 | solution.py:296
  14.8 0.2 fetch.2
  15.0 10.7 %all_to_all.28.refs_0_ = f32[8,1,128,128]{3,2,1,0:T(8,128)S(1)} all-to-all(f32[8,1,128,128]{3,2,1,0:T(8,128)S(1)} %get-tuple-element.30), channel_id=1, replica_groups={{0,2,4,6,8,10,12,14},{16,18,20,22,24,26,28,30},{1,3,5,7,9,11,13,15},{17..., dimensions={0} | all-to-all | bytes 1048576 | tf_op jit(solution)/shard_map/cond/branch_1_fun/all_to_all | solution.py:247
  25.7 0.5 %first.1 = (f32[8,1,128]{2,1,0:T(1,128)S(1)}, f32[1,128]{1,0:T(1,128)S(1)}) custom-call(f32[8,1,128,128]{3,2,1,0:T(8,128)S(1)} %all_to_all.28.refs_0_, f32[8,128]{1,0:T(8,128)S(1)} %get-tuple-element.64.refs_1_), custom_call_target="tpu_custom_call" | custom-call | tf_op jit(solution)/shard_map/cond/branch_1_fun/first/pallas_call | solution.py:211
  26.2 1.3 %collective-permute-start = (f32[1,128]{1,0:T(1,128)S(1)}, f32[1,128]{1,0:T(1,128)S(1)}, u32[]{:S(2)}, u32[]{:S(2)}) collective-permute-start(f32[1,128]{1,0:T(1,128)S(1)} %get-tuple-element.59), channel_id=1, source_target_pairs={{0,16},{2,18},{4,20},{6,22},{8,24},{10,26},{12,28},{14,30},{1,17},... | collective-permute-start | bytes 1544 | tf_op jit(solution)/shard_map/ppermute | solution.py:300
  27.5 8.0 %conditional.3 = (f32[32,128]{1,0:T(8,128)S(1)}, f32[8,2,128,128]{3,2,1,0:T(8,128)S(1)}) conditional(s32[]{:T(128)} %convert_element_type.4, (s32[16,1,8]{2,1,0:T(1,128)S(1)}, s32[1,8]{1,0:T(1,128)S(1)}, s32[1,8]{1,0:T(1,128)S(1)}, bf16[64,128,128]{2,1,0:T(8,128)(2,1)S(1)}) %tuple.38, (f32[8,1,128]{2,1,0:T(1,128)S(1)}, s32[2,8]{1,0:T(2,128)S(1)}, ...), branch_computations={%region_2.3_spmd, %region_3.4_spmd} | conditional | bytes 2113556 | solution.py:301
  27.5 7.5 %all_to_all.30.refs_0_ = f32[8,1,128]{2,1,0:T(1,128)S(1)} all-to-all(f32[8,1,128]{2,1,0:T(1,128)S(1)} %get-tuple-element.40), channel_id=1, replica_groups={{4,2,0,6,8,10,12,14},{20,18,16,22,24,26,28,30},{5,3,1,7,9,11,13,15},{21..., dimensions={0} | all-to-all | bytes 8192 | tf_op jit(solution)/shard_map/cond/branch_1_fun/all_to_all | solution.py:247
  35.0 0.4 site_weights.1
  35.4 0.1 broadcast.16
  35.5 0.0 collective-permute-done.refs_2_
  35.5 8.8 %all_to_all.31 = f32[32,1,128]{2,1,0:T(1,128)S(1)} all-to-all(f32[32,1,128]{2,1,0:T(1,128)S(1)} %bitcast.10), channel_id=1, replica_groups=mesh['site'=16,'batch'=2] {'batch','site'}, dimensions={0} | all-to-all | bytes 32768 | tf_op jit(solution)/shard_map/all_to_all | solution.py:324
  44.3 0.6 %collect.1 = (f32[1,8]{1,0:T(1,128)}, f32[1,8]{1,0:T(1,128)}, f32[1,1]{1,0:T(1,128)}) custom-call(f32[32,128]{1,0:T(8,128)S(1)} %bitcast.11), custom_call_target="tpu_custom_call" | custom-call | tf_op jit(solution)/shard_map/collect/pallas_call | solution.py:211
  (1 shorter events, 0.0 us)
Async XLA Ops:
  1.9 12.9 %all-to-all-start.3 = ((s32[16,1,8]{2,1,0:T(1,128)}), s32[16,1,8]{2,1,0:T(1,128)S(1)}, u32[]{:S(2)}, u32[]{:S(2)}) async-start(s32[16,1,8]{2,1,0:T(1,128)} %broadcast_in_dim.12), calls=%async_computation.3 | async-start | bytes 16384 | tf_op jit(solution)/shard_map/all_to_all | solution.py:239
  10.7 1.6 %copy-start = (bf16[1,2,32,128,128]{4,3,2,1,0:T(8,128)(2,1)S(1)}, bf16[1,2,32,128,128]{4,3,2,1,0:T(8,128)(2,1)}, u32[]{:S(2)}) copy-start(bf16[1,2,32,128,128]{4,3,2,1,0:T(8,128)(2,1)} %param.8) | copy-start | bytes 6291460
  12.3 2.5 %copy-start.1 = (s32[1,8]{1,0:T(1,128)S(1)}, s32[1,8]{1,0:T(1,128)}, u32[]{:S(2)}) copy-start(s32[1,8]{1,0:T(1,128)} %param.11) | copy-start | bytes 100
  12.3 2.5 %copy-start.2 = (f32[8,128]{1,0:T(8,128)S(1)}, f32[8,128]{1,0:T(8,128)}, u32[]{:S(2)}) copy-start(f32[8,128]{1,0:T(8,128)} %param.9) | copy-start | bytes 12292
  12.3 2.5 %copy-start.3 = (s32[8]{0:T(128)S(1)}, s32[8]{0:T(128)}, u32[]{:S(2)}) copy-start(s32[8]{0:T(128)} %param.10) | copy-start | bytes 100
  26.2 9.3 %collective-permute-start = (f32[1,128]{1,0:T(1,128)S(1)}, f32[1,128]{1,0:T(1,128)S(1)}, u32[]{:S(2)}, u32[]{:S(2)}) collective-permute-start(f32[1,128]{1,0:T(1,128)S(1)} %get-tuple-element.59), channel_id=1, source_target_pairs={{0,16},{2,18},{4,20},{6,22},{8,24},{10,26},{12,28},{14,30},{1,17},... | collective-permute-start | bytes 1544 | tf_op jit(solution)/shard_map/ppermute | solution.py:300
